TPU v7x, 32 devices: a whole 2x2x4 slice. The times are simulated.
32 devices in a mesh: fsdp: 8 (over z, x), dp: 4 (over y, core).
Axes of the slice: x: 2, y: 2, z: 4, core: 2. Of those that a mesh axis runs over, the one named last changes fastest.
Arguments:
- patches: bfloat16 [160, 197, 768], P(('fsdp', 'dp')), may hold values from -6 to 6
- keep: int32 [160, 197], P(('fsdp', 'dp')), may hold values from -1 to 196, as said below
- ln1_gain: bfloat16 [768], P('fsdp'), may hold values from 0.5 to 1.5
- ln1_bias: bfloat16 [768], P('fsdp'), may hold values from -1.1953125 to 1.1953125
- w_qkv: bfloat16 [768, 2304], P('fsdp'), may hold values from -0.21875 to 0.21875
- b_query: bfloat16 [768], P('fsdp'), may hold values from -1.1953125 to 1.1953125
- b_value: bfloat16 [768], P('fsdp'), may hold values from -1.1953125 to 1.1953125
- w_out: bfloat16 [768, 768], P('fsdp'), may hold values from -1.75 to 1.75
- b_out: bfloat16 [768], P('fsdp'), may hold values from -1.1953125 to 1.1953125
- ln2_gain: bfloat16 [768], P('fsdp'), may hold values from 0.5 to 1.5
- ln2_bias: bfloat16 [768], P('fsdp'), may hold values from -1.1953125 to 1.1953125
- w_up: bfloat16 [768, 3072], P('fsdp'), may hold values from -0.21875 to 0.21875
- b_up: bfloat16 [3072], P('fsdp'), may hold values from -1.1953125 to 1.1953125
- w_down: bfloat16 [3072, 768], P('fsdp'), may hold values from -0.109375 to 0.109375
- b_down: bfloat16 [768], P('fsdp'), may hold values from -1.1953125 to 1.1953125
- cotangent: bfloat16 [160, 197, 768], P(('fsdp', 'dp')), may hold values from -6 to 6
Outputs:
- out_tokens: bfloat16 [160, 197, 768], P(('fsdp', 'dp'))
- grad_patches: float32 [160, 197, 768], P(('fsdp', 'dp'))
- g_ln1_gain: float32 [768], P('fsdp')
- g_ln1_bias: float32 [768], P('fsdp')
- g_w_qkv: float32 [768, 2304], P('fsdp')
- g_b_query: float32 [768], P('fsdp')
- g_b_value: float32 [768], P('fsdp')
- g_w_out: float32 [768, 768], P('fsdp')
- g_b_out: float32 [768], P('fsdp')
- g_ln2_gain: float32 [768], P('fsdp')
- g_ln2_bias: float32 [768], P('fsdp')
- g_w_up: float32 [768, 3072], P('fsdp')
- g_b_up: float32 [3072], P('fsdp')
- g_w_down: float32 [3072, 768], P('fsdp')
- g_b_down: float32 [768], P('fsdp')
Inputs may be any that keep to these rules, and one draw needn't show every extreme that they name: `keep`: each row holds the class token 0 first, then that image's kept patch positions in rising order, then -1 in the remaining slots. Every image keeps 197 // 4 or more positions, and some image keeps all 197.
All inputs are finite; a program needn't handle non-finite values.
Results may differ from a plain program's by a relative error of at most 0.018.
Values may be sent and summed in bfloat16 or wider, within the bound.
A program may use at most 192 MiB of HBM per device.

v0:
```python
import math

import jax
import jax.numpy as jnp
from jax import lax
from jax.sharding import PartitionSpec as P

H = 12
HD = 64


EPSILON = 1e-06


def layer_norm(values, gain, shift):
    centre = values - jnp.mean(values, axis=-1, keepdims=True)
    spread = jnp.mean(centre * centre, axis=-1, keepdims=True)
    return centre * lax.rsqrt(spread + EPSILON) * gain + shift


def exact_gelu(values):
    return jax.nn.gelu(values, approximate=False)


def contract_rows(left, right):
    return lax.dot_general(
        left, right, (((0,), (0,)), ((), ())), preferred_element_type=jnp.float32
    )


def times_transpose(left, right):
    return lax.dot_general(
        left, right, (((1,), (1,)), ((), ())), preferred_element_type=jnp.float32
    )


def column_sums(values):
    return jnp.sum(values.astype(jnp.float32), axis=0)


def shards(
    patches,
    keep,
    ln1_gain,
    ln1_bias,
    w_qkv,
    b_query,
    b_value,
    w_out,
    b_out,
    ln2_gain,
    ln2_bias,
    w_up,
    b_up,
    w_down,
    b_down,
    cotangent,
):
    images, slots = keep.shape
    width = patches.shape[2]
    row_count = images * slots
    factor = 1.0 / math.sqrt(HD)
    live_slots = keep >= 0
    live_rows = live_slots.reshape(row_count, 1).astype(jnp.float32)
    slot_index = jnp.maximum(keep, 0)
    tokens_in = jnp.take_along_axis(patches, slot_index[..., None], axis=1)
    tokens_in = tokens_in.reshape(row_count, width).astype(jnp.float32)
    attn_set = (
        lax.all_gather(ln1_gain, "fsdp", axis=0, tiled=True),
        lax.all_gather(ln1_bias, "fsdp", axis=0, tiled=True),
        lax.all_gather(w_qkv, "fsdp", axis=0, tiled=True),
        lax.all_gather(b_query, "fsdp", axis=0, tiled=True),
        lax.all_gather(b_value, "fsdp", axis=0, tiled=True),
        lax.all_gather(w_out, "fsdp", axis=0, tiled=True),
        lax.all_gather(b_out, "fsdp", axis=0, tiled=True),
    )
    gain_one, shift_one, qkv_full, query_bias, value_bias, out_full, out_bias = attn_set
    normed_one, norm_pull_one = jax.vjp(
        layer_norm, tokens_in, gain_one.astype(jnp.float32), shift_one.astype(jnp.float32)
    )
    normed_low = normed_one.astype(jnp.bfloat16)
    bias_all = jnp.concatenate([query_bias, jnp.zeros_like(query_bias), value_bias]).astype(
        jnp.float32
    )
    projected = (
        jnp.dot(normed_low, qkv_full, preferred_element_type=jnp.float32) + bias_all
    ).astype(jnp.bfloat16)
    queries = projected[:, :width].reshape(images, slots, H, HD)
    key_heads = projected[:, width : 2 * width].reshape(images, slots, H, HD)
    value_heads = projected[:, 2 * width :].reshape(images, slots, H, HD)

    def scores_of():
        raw_scores = (
            jnp.einsum("iqhd,ikhd->ihqk", queries, key_heads, preferred_element_type=jnp.float32)
            * factor
        )
        return jnp.where(live_slots[:, None, None, :], raw_scores, -1e30)

    scores = scores_of()
    highest = jnp.max(scores, axis=-1, keepdims=True)
    exponent = jnp.exp(scores - highest)
    totals = jnp.sum(exponent, axis=-1, keepdims=True)
    log_total = highest + jnp.log(totals)
    attention_low = (exponent / totals).astype(jnp.bfloat16)
    attended = jnp.einsum(
        "ihqk,ikhd->iqhd", attention_low, value_heads, preferred_element_type=jnp.float32
    )
    attended = attended.astype(jnp.bfloat16).reshape(row_count, width)
    middle = (
        tokens_in
        + jnp.dot(attended, out_full, preferred_element_type=jnp.float32)
        + out_bias.astype(jnp.float32)
    )
    mlp_set = (
        lax.all_gather(ln2_gain, "fsdp", axis=0, tiled=True),
        lax.all_gather(ln2_bias, "fsdp", axis=0, tiled=True),
        lax.all_gather(w_up, "fsdp", axis=0, tiled=True),
        lax.all_gather(b_up, "fsdp", axis=0, tiled=True),
        lax.all_gather(w_down, "fsdp", axis=0, tiled=True),
        lax.all_gather(b_down, "fsdp", axis=0, tiled=True),
    )
    gain_two, shift_two, up_full, up_bias, down_full, down_bias = mlp_set
    normed_two, norm_pull_two = jax.vjp(
        layer_norm, middle, gain_two.astype(jnp.float32), shift_two.astype(jnp.float32)
    )
    normed_two_low = normed_two.astype(jnp.bfloat16)
    hidden = jnp.dot(normed_two_low, up_full, preferred_element_type=jnp.float32) + up_bias.astype(
        jnp.float32
    )
    activated, gelu_pull = jax.vjp(exact_gelu, hidden)
    activated_low = activated.astype(jnp.bfloat16)
    final = (
        middle
        + jnp.dot(activated_low, down_full, preferred_element_type=jnp.float32)
        + down_bias.astype(jnp.float32)
    ) * live_rows
    out_tokens = final.astype(jnp.bfloat16).reshape(images, slots, width)
    up_back, down_back = (
        lax.all_gather(w_up, "fsdp", axis=0, tiled=True),
        lax.all_gather(w_down, "fsdp", axis=0, tiled=True),
    )
    grad_final = cotangent.astype(jnp.float32).reshape(row_count, width) * live_rows
    grad_mixed_low = grad_final.astype(jnp.bfloat16)
    grad_down = contract_rows(activated_low, grad_mixed_low)
    grad_down_bias = column_sums(grad_mixed_low)
    (grad_hidden,) = gelu_pull(times_transpose(grad_mixed_low, down_back))
    grad_hidden_low = grad_hidden.astype(jnp.bfloat16)
    grad_up = contract_rows(normed_two_low, grad_hidden_low)
    grad_up_bias = column_sums(grad_hidden_low)
    grad_middle_norm, grad_gain_two, grad_shift_two = norm_pull_two(
        times_transpose(grad_hidden_low, up_back)
    )
    mlp_grads = (
        lax.psum_scatter(
            grad_gain_two.astype(jnp.bfloat16), "fsdp", scatter_dimension=0, tiled=True
        ).astype(jnp.float32),
        lax.psum_scatter(
            grad_shift_two.astype(jnp.bfloat16), "fsdp", scatter_dimension=0, tiled=True
        ).astype(jnp.float32),
        lax.psum_scatter(
            grad_up.astype(jnp.bfloat16), "fsdp", scatter_dimension=0, tiled=True
        ).astype(jnp.float32),
        lax.psum_scatter(
            grad_up_bias.astype(jnp.bfloat16), "fsdp", scatter_dimension=0, tiled=True
        ).astype(jnp.float32),
        lax.psum_scatter(
            grad_down.astype(jnp.bfloat16), "fsdp", scatter_dimension=0, tiled=True
        ).astype(jnp.float32),
        lax.psum_scatter(
            grad_down_bias.astype(jnp.bfloat16), "fsdp", scatter_dimension=0, tiled=True
        ).astype(jnp.float32),
    )
    grad_middle = grad_final + grad_middle_norm
    qkv_back, out_back = (
        lax.all_gather(w_qkv, "fsdp", axis=0, tiled=True),
        lax.all_gather(w_out, "fsdp", axis=0, tiled=True),
    )
    grad_branch_low = grad_middle.astype(jnp.bfloat16)
    grad_out = contract_rows(attended, grad_branch_low)
    grad_out_bias = column_sums(grad_branch_low)
    grad_attended = (
        times_transpose(grad_branch_low, out_back)
        .astype(jnp.bfloat16)
        .reshape(images, slots, H, HD)
    )
    recomputed = jnp.exp(scores_of() - log_total)
    recomputed_low = recomputed.astype(jnp.bfloat16)
    grad_values = jnp.einsum(
        "ihqk,iqhd->ikhd", recomputed_low, grad_attended, preferred_element_type=jnp.float32
    )
    grad_weights = jnp.einsum(
        "iqhd,ikhd->ihqk", grad_attended, value_heads, preferred_element_type=jnp.float32
    )
    grad_scores = recomputed * (
        grad_weights - jnp.sum(recomputed * grad_weights, axis=-1, keepdims=True)
    )
    grad_scores_low = grad_scores.astype(jnp.bfloat16)
    grad_queries = (
        jnp.einsum(
            "ihqk,ikhd->iqhd", grad_scores_low, key_heads, preferred_element_type=jnp.float32
        )
        * factor
    )
    grad_keys = (
        jnp.einsum("ihqk,iqhd->ikhd", grad_scores_low, queries, preferred_element_type=jnp.float32)
        * factor
    )
    grad_projected = jnp.concatenate(
        [
            grad_queries.reshape(row_count, width),
            grad_keys.reshape(row_count, width),
            grad_values.reshape(row_count, width),
        ],
        axis=1,
    ).astype(jnp.bfloat16)
    grad_qkv = contract_rows(normed_low, grad_projected)
    grad_query_bias = column_sums(grad_projected[:, :width])
    grad_value_bias = column_sums(grad_projected[:, 2 * width :])
    grad_tokens_norm, grad_gain_one, grad_shift_one = norm_pull_one(
        times_transpose(grad_projected, qkv_back)
    )
    attn_grads = (
        lax.psum_scatter(
            grad_gain_one.astype(jnp.bfloat16), "fsdp", scatter_dimension=0, tiled=True
        ).astype(jnp.float32),
        lax.psum_scatter(
            grad_shift_one.astype(jnp.bfloat16), "fsdp", scatter_dimension=0, tiled=True
        ).astype(jnp.float32),
        lax.psum_scatter(
            grad_qkv.astype(jnp.bfloat16), "fsdp", scatter_dimension=0, tiled=True
        ).astype(jnp.float32),
        lax.psum_scatter(
            grad_query_bias.astype(jnp.bfloat16), "fsdp", scatter_dimension=0, tiled=True
        ).astype(jnp.float32),
        lax.psum_scatter(
            grad_value_bias.astype(jnp.bfloat16), "fsdp", scatter_dimension=0, tiled=True
        ).astype(jnp.float32),
        lax.psum_scatter(
            grad_out.astype(jnp.bfloat16), "fsdp", scatter_dimension=0, tiled=True
        ).astype(jnp.float32),
        lax.psum_scatter(
            grad_out_bias.astype(jnp.bfloat16), "fsdp", scatter_dimension=0, tiled=True
        ).astype(jnp.float32),
    )
    grad_tokens = (grad_middle + grad_tokens_norm) * live_rows
    image_rows = jnp.arange(images, dtype=jnp.int32)[:, None]
    grad_patches = (
        jnp.zeros(patches.shape, jnp.float32)
        .at[image_rows, slot_index]
        .add(grad_tokens.reshape(images, slots, width))
    )
    gain_one_sum, shift_one_sum, qkv_sum, query_sum, value_sum, out_sum, out_bias_sum = attn_grads
    gain_two_sum, shift_two_sum, up_sum, up_bias_sum, down_sum, down_bias_sum = mlp_grads
    totals_all = (
        lax.psum(gain_one_sum.astype(jnp.bfloat16), "dp").astype(jnp.float32),
        lax.psum(shift_one_sum.astype(jnp.bfloat16), "dp").astype(jnp.float32),
        lax.psum(qkv_sum.astype(jnp.bfloat16), "dp").astype(jnp.float32),
        lax.psum(query_sum.astype(jnp.bfloat16), "dp").astype(jnp.float32),
        lax.psum(value_sum.astype(jnp.bfloat16), "dp").astype(jnp.float32),
        lax.psum(out_sum.astype(jnp.bfloat16), "dp").astype(jnp.float32),
        lax.psum(out_bias_sum.astype(jnp.bfloat16), "dp").astype(jnp.float32),
        lax.psum(gain_two_sum.astype(jnp.bfloat16), "dp").astype(jnp.float32),
        lax.psum(shift_two_sum.astype(jnp.bfloat16), "dp").astype(jnp.float32),
        lax.psum(up_sum.astype(jnp.bfloat16), "dp").astype(jnp.float32),
        lax.psum(up_bias_sum.astype(jnp.bfloat16), "dp").astype(jnp.float32),
        lax.psum(down_sum.astype(jnp.bfloat16), "dp").astype(jnp.float32),
        lax.psum(down_bias_sum.astype(jnp.bfloat16), "dp").astype(jnp.float32),
    )
    return (
        out_tokens,
        grad_patches,
        totals_all[0],
        totals_all[1],
        totals_all[2],
        totals_all[3],
        totals_all[4],
        totals_all[5],
        totals_all[6],
        totals_all[7],
        totals_all[8],
        totals_all[9],
        totals_all[10],
        totals_all[11],
        totals_all[12],
    )


def solution(mesh):
    in_specs = (
        P(("fsdp", "dp"), None, None),
        P(("fsdp", "dp"), None),
        P("fsdp"),
        P("fsdp"),
        P("fsdp", None),
        P("fsdp"),
        P("fsdp"),
        P("fsdp", None),
        P("fsdp"),
        P("fsdp"),
        P("fsdp"),
        P("fsdp", None),
        P("fsdp"),
        P("fsdp", None),
        P("fsdp"),
        P(("fsdp", "dp"), None, None),
    )
    out_specs = (
        P(("fsdp", "dp"), None, None),
        P(("fsdp", "dp"), None, None),
        P("fsdp"),
        P("fsdp"),
        P("fsdp", None),
        P("fsdp"),
        P("fsdp"),
        P("fsdp", None),
        P("fsdp"),
        P("fsdp"),
        P("fsdp"),
        P("fsdp", None),
        P("fsdp"),
        P("fsdp", None),
        P("fsdp"),
    )
    return jax.shard_map(shards, mesh=mesh, in_specs=in_specs, out_specs=out_specs, check_vma=False)
```

profile of v0, /device:TPU:1, one launch (start us, length us, event | category | flops | bytes accessed | tf_op | source)
XLA Modules:
  0.0 899.5 jit_solution(2613318900690820602)
XLA Ops:
  10.1 1.3 fusion.33
  12.2 11.8 %gather_fusion = bf16[985,768]{1,0:T(8,128)(2,1)S(1)} fusion(bf16[5,197,768]{2,1,0:T(8,128)(2,1)S(1)} %copy-done, s32[985]{0:T(1024)S(1)} %reshape.236), kind=kCustom, calls=%fused_computation | custom fusion | bytes 3033800 | tf_op jit(solution)/shard_map/jit(take_along_axis)/gather | solution.py:66
  29.0 31.8 %all-reduce.18 = (bf16[768]{0:T(1024)(128)(2,1)S(1)}, bf16[768]{0:T(1024)(128)(2,1)S(1)}, bf16[768]{0:T(1024)(128)(2,1)S(1)}, bf16[768]{0:T(1024)(128)(2,1)S(1)}...) all-reduce(bf16[768]{0:T(1024)(128)(2,1)S(1)} %dynamic-update-slice, ...), channel_id=1, replica_groups=mesh['fsdp'=8,'dp'=4] {'fsdp'}, use_global_device_ids=true, to_apply=%add.3 | all-reduce | flops 5376 | bytes 21504
  61.0 22.3 %all-gather = bf16[8,1,384]{2,1,0:T(2,128)(2,1)S(1)} all-gather(bf16[1,1,384]{2,1,0:T(2,128)(2,1)S(1)} %reshape.274), channel_id=1, replica_groups=mesh['fsdp'=8,'dp'=4] {'fsdp'}, dimensions={0}, use_global_device_ids=true | all-gather | bytes 6912 | tf_op jit(solution)/shard_map/all_gather | solution.py:118
  83.4 3.4 reshape.227
  86.9 6.6 add_convert_fusion.1
  93.6 1.9 fusion.50
  95.5 5.8 reshape.302
  101.3 6.0 copy.68
  107.3 5.8 reshape.303
  113.1 6.1 copy.66
  119.1 4.3 reshape.304
  123.4 6.4 copy.67
  129.8 5.4 fusion.12
  135.2 3.7 fusion.6
  140.0 3.4 convert_bitcast_fusion.1
  143.4 3.2 copy.70
  146.6 5.7 reshape.225
  152.3 3.5 fusion.52
  155.8 1.6 copy-done.9
  158.6 41.5 %all-gather.10.cloned.1.call-done = bf16[768,3072]{1,0:T(8,128)(2,1)} async-done(((bf16[96,3072]{1,0:T(8,128)(2,1)}), bf16[768,3072]{1,0:T(8,128)(2,1)}) %all-gather.10.cloned.1.call-update) | async-done | bytes 4718608 | tf_op jit(solution)/shard_map/all_gather | solution.py:117
  200.1 36.7 %multiply_convert_fusion.1 = (bf16[985,3072]{1,0:T(8,128)(2,1)}, f32[985,3072]{1,0:T(8,128)}, f32[985,3072]{1,0:T(8,128)}) fusion(f32[3072]{0:T(1024)S(1)} %bitcast.58, bf16[768,3072]{1,0:T(8,128)(2,1)} %all-gather.10.cloned.1.call-done, f32[985,768]{1,0:T(8,128)} %copy-done.9, f32[768]{0:T(1024)S(1)} %convert_element_type.209, ...), kind=kOutput, calls=%fused_computation.11 | convolution fusion | flops 4851306496 | bytes 38030024 | tf_op jit(solution)/shard_map/dot_general | solution.py:127
  236.8 43.4 %all-gather.12.cloned.1.call-done = bf16[3072,768]{1,0:T(8,128)(2,1)} async-done(((bf16[384,768]{1,0:T(8,128)(2,1)}), bf16[3072,768]{1,0:T(8,128)(2,1)}) %all-gather.12.cloned.1.call-update) | async-done | bytes 4718608 | tf_op jit(solution)/shard_map/all_gather | solution.py:119
  280.2 18.6 %fusion.55 = (bf16[3072]{0:T(1024)(128)(2,1)S(1)}, bf16[985,3072]{1,0:T(8,128)(2,1)}) fusion(f32[985,3072]{1,0:T(8,128)} %get-tuple-element.59, bf16[3072,768]{1,0:T(8,128)(2,1)} %all-gather.12.cloned.1.call-done, f32[985,768]{1,0:T(8,128)} %reshape.227, f32[985]{0:T(1024)S(1)} %reshape.235, f32[985,3072]{1,0:T(8,128)} %get-tuple-element.72, ...), kind=kOutput, calls=%fused_computation.115 | convolution fusion | flops 4697737728 | bytes 38026084 | tf_op jit(solution)/shard_map/dot_general | solution.py:32
  298.8 10.6 %multiply_reduce_fusion.1 = (bf16[768]{0:T(1024)(128)(2,1)S(1)}, f32[985]{0:T(1024)S(1)}, bf16[768]{0:T(1024)(128)(2,1)S(1)}, f32[985,768]{1,0:T(8,128)S(1)}) fusion(f32[985,768]{1,0:T(8,128)} %copy-done.9, f32[985]{0:T(1024)S(1)} %fusion.34, f32[985]{0:T(1024)S(1)} %broadcast_multiply_fusion.1, f32[768]{0:T(1024)S(1)} %convert_element_type.208, ...), kind=kOutput, calls=%fused_computation.56 | convolution fusion | flops 4653862912 | bytes 16840236 | tf_op jit(solution)/shard_map/dot_general | solution.py:32
  309.5 1.9 fusion.47
  311.9 1.6 copy-done.8
  313.5 2.4 convolution_convert_fusion.4
  315.9 3.3 convolution_convert_fusion.3
  319.2 4.3 reshape.305
  323.5 6.2 copy.72
  329.7 9.6 %multiply_reduce_fusion = (f32[5,12,197]{2,1,0:T(8,128)S(1)}, f32[5,12,197,197]{2,3,1,0:T(8,128)S(1)}) fusion(f32[5,12,197]{2,1,0:T(8,128)S(1)} %copy-done.23, f32[5,12,197,197]{2,3,1,0:T(8,128)} %copy-done.2, pred[5,197]{1,0:T(8,128)(4,1)S(1)} %copy-done.29, bf16[5,197,12,64]{1,3,2,0:T(8,128)(2,1)} %copy.72, bf16[5,197,12,64]{1,3,2,0:T(8,128)(2,1)S(1)} %copy-done.16), kind=kOutput, calls=%fused_computation.4 | convolution fusion | flops 309684032 | bytes 21749784 | tf_op jit(solution)/shard_map/iqhd,ikhd->ihqk/dot_general | solution.py:191
  339.3 7.2 multiply_convert_fusion
  346.5 2.6 copy-done.3
  349.1 2.6 fusion.53
  351.8 6.3 fusion.28
  358.2 3.2 copy.76
  361.3 5.7 reshape.229
  367.0 3.2 copy.79
  370.2 5.7 reshape.230
  375.8 7.7 fusion.54
  383.6 3.1 copy.82
  386.7 5.9 reshape.231
  392.7 1.3 copy-done.19
  394.6 2.1 copy-done.25
  396.8 6.4 convolution_convert_fusion.2
  403.2 10.4 %convolution_convert_fusion.1 = bf16[768,3072]{1,0:T(8,128)(2,1)} fusion(bf16[985,3072]{1,0:T(8,128)(2,1)} %get-tuple-element.82, f32[985,768]{1,0:T(8,128)} %copy-done.9, f32[768]{0:T(1024)S(1)} %convert_element_type.209, f32[768]{0:T(1024)S(1)} %convert_element_type.208, f32[985]{0:T(1024)S(1)} %fusion.34, f32[985]{0:T(1024)S(1)} %broadcast_multiply_fusion.1), kind=kOutput, calls=%fused_computation.32 | convolution fusion | flops 4653955072 | bytes 13810376 | tf_op jit(solution)/shard_map/dot_general | solution.py:26
  413.7 9.8 %convolution_convert_fusion = bf16[3072,768]{1,0:T(8,128)(2,1)} fusion(bf16[985,3072]{1,0:T(8,128)(2,1)} %get-tuple-element.58, f32[985,768]{1,0:T(8,128)} %reshape.227, f32[985]{0:T(1024)S(1)} %reshape.235), kind=kOutput, calls=%fused_computation.31 | convolution fusion | flops 4651685376 | bytes 13800292 | tf_op jit(solution)/shard_map/dot_general | solution.py:26
  426.7 7.9 fusion.46
  434.6 1.6 copy-done.12
  436.1 1.9 fusion.22
  438.0 29.5 %all-reduce.17 = (bf16[768]{0:T(1024)(128)(2,1)S(1)}, bf16[768]{0:T(1024)(128)(2,1)S(1)}, bf16[768]{0:T(1024)(128)(2,1)S(1)}, bf16[768]{0:T(1024)(128)(2,1)S(1)}...) all-reduce(bf16[768]{0:T(1024)(128)(2,1)S(1)} %dynamic-update-slice, ...), channel_id=1, replica_groups=mesh['fsdp'=8,'dp'=4] {'fsdp'}, use_global_device_ids=true, to_apply=%add.7 | all-reduce | flops 9984 | bytes 39936
  467.5 29.6 %reduce-scatter.5.cloned.1.call-done = bf16[96,2304]{1,0:T(8,128)(2,1)} async-done(((bf16[768,2304]{1,0:T(8,128)(2,1)}), bf16[96,2304]{1,0:T(8,128)(2,1)}) %reduce-scatter.5.cloned.1.call-update) | async-done | bytes 442384 | tf_op jit(solution)/shard_map/reduce_scatter | solution.py:229
  497.2 98.7 %reduce-scatter.9.cloned.1.call-done = bf16[96,3072]{1,0:T(8,128)(2,1)} async-done(((bf16[768,3072]{1,0:T(8,128)(2,1)}), bf16[96,3072]{1,0:T(8,128)(2,1)}) %reduce-scatter.9.cloned.1.call-update) | async-done | bytes 589840 | tf_op jit(solution)/shard_map/reduce_scatter | solution.py:160
  595.9 98.7 %reduce-scatter.11.cloned.1.call-done = bf16[384,768]{1,0:T(8,128)(2,1)} async-done(((bf16[3072,768]{1,0:T(8,128)(2,1)}), bf16[384,768]{1,0:T(8,128)(2,1)}) %reduce-scatter.11.cloned.1.call-update) | async-done | bytes 589840 | tf_op jit(solution)/shard_map/reduce_scatter | solution.py:166
  694.6 9.9 %multiply_convert_fusion.5 = bf16[985,768]{1,0:T(8,128)(2,1)S(1)} fusion(f32[985,768]{1,0:T(8,128)} %copy-done.9, bf16[985,3072]{1,0:T(8,128)(2,1)} %get-tuple-element.58, bf16[3072,768]{1,0:T(8,128)(2,1)} %all-gather.12.cloned.1.call-done, f32[985]{0:T(1024)S(1)} %reshape.235, f32[768]{0:T(1024)S(1)} %convert_element_type.213), kind=kOutput, calls=%fused_computation.60 | convolution fusion | flops 4650840064 | bytes 15316324 | tf_op jit(solution)/shard_map/dot_general | solution.py:134
  704.5 1.6 reshape.226
  706.8 6.2 all-reduce.19
  717.6 4.7 add_multiply_fusion
  722.3 1.8 broadcast_in_dim.81
  724.2 161.4 %scatter_fusion = f32[5,197,768]{2,1,0:T(8,128)} fusion(f32[5,197,768]{2,1,0:T(8,128)} %broadcast_in_dim.81, s32[985]{0:T(1024)S(1)} %reshape.242, f32[985,768]{1,0:T(8,128)} %add_multiply_fusion), kind=kCustom, calls=%fused_computation.1 | custom fusion | flops 756480 | bytes 9085640 | tf_op jit(solution)/shard_map/scatter-add | solution.py:250
  885.6 2.0 convert_element_type.229
  887.7 1.6 convert_element_type.233
  889.3 2.2 convert_element_type.240
  (198 shorter events, 20.1 us)
Async XLA Ops:
  7.2 5.0 copy-start
  7.2 79.7 %all-gather.6.cloned.1.call-start = ((), (), s32[]{:S(2)}) async-start(), calls=%async_computation.4 | async-start | bytes 3981312 | tf_op jit(solution)/shard_map/all_gather | solution.py:71
  7.9 144.4 %all-gather.8.cloned.1.call-start = ((), (), s32[]{:S(2)}) async-start(), calls=%async_computation.5 | async-start | bytes 1327104 | tf_op jit(solution)/shard_map/all_gather | solution.py:74
  8.7 191.4 %all-gather.10.cloned.1.call-start = ((), (), s32[]{:S(2)}) async-start(), calls=%async_computation.6 | async-start | bytes 5308416 | tf_op jit(solution)/shard_map/all_gather | solution.py:117
  9.4 270.8 %all-gather.12.cloned.1.call-start = ((), (), s32[]{:S(2)}) async-start(), calls=%async_computation.7 | async-start | bytes 5308416 | tf_op jit(solution)/shard_map/all_gather | solution.py:119
  10.0 457.5 %reduce-scatter.7.cloned.1.call-start = ((), (), s32[]{:S(2)}) async-start(), calls=%async_computation.9 | async-start | bytes 1327104 | tf_op jit(solution)/shard_map/reduce_scatter | solution.py:238
  12.1 71.3 %copy-start.26 = (f32[5,197]{1,0:T(8,128)}, f32[5,197]{1,0:T(8,128)S(1)}, u32[]{:S(2)}) copy-start(f32[5,197]{1,0:T(8,128)S(1)} %get-tuple-element.56) | copy-start | bytes 11824
  12.1 126.9 %copy-start.28 = (pred[5,197]{1,0:T(8,128)(4,1)}, pred[5,197]{1,0:T(8,128)(4,1)S(1)}, u32[]{:S(2)}) copy-start(pred[5,197]{1,0:T(8,128)(4,1)S(1)} %get-tuple-element.57) | copy-start | bytes 2959
  24.0 128.3 %copy-start.4 = (bf16[985,768]{1,0:T(8,128)(2,1)}, bf16[985,768]{1,0:T(8,128)(2,1)S(1)}, u32[]{:S(2)}) copy-start(bf16[985,768]{1,0:T(8,128)(2,1)S(1)} %gather_fusion) | copy-start | bytes 4538884
  24.0 2.1 copy-start.43
  24.0 3.3 copy-start.46
  24.0 3.6 copy-start.47
  24.0 3.8 copy-start.48
  24.1 4.0 copy-start.49
  24.1 4.2 copy-start.50
  24.1 4.5 copy-start.51
  24.1 4.7 copy-start.52
  24.1 36.8 %copy-start.44 = (bf16[384]{0:T(512)(128)(2,1)S(1)}, bf16[384]{0:T(512)(128)(2,1)}, u32[]{:S(2)}) copy-start(bf16[384]{0:T(512)(128)(2,1)} %param.28) | copy-start | bytes 2308
  26.0 60.9 %copy-start.32 = (f32[985]{0:T(1024)}, f32[985]{0:T(1024)S(1)}, u32[]{:S(2)}) copy-start(f32[985]{0:T(1024)S(1)} %div.47) | copy-start | bytes 11824
  26.1 126.2 %copy-start.39 = (pred[985]{0:T(1024)(128)(4,1)}, pred[985]{0:T(1024)(128)(4,1)S(1)}, u32[]{:S(2)}) copy-start(pred[985]{0:T(1024)(128)(4,1)S(1)} %broadcast_in_dim.73) | copy-start | bytes 2959
  60.8 32.8 %copy-start.41 = (f32[768]{0:T(1024)}, f32[768]{0:T(1024)S(1)}, u32[]{:S(2)}) copy-start(f32[768]{0:T(1024)S(1)} %convert_element_type.200) | copy-start | bytes 9220
  60.8 32.8 %copy-start.34 = (f32[768]{0:T(1024)}, f32[768]{0:T(1024)S(1)}, u32[]{:S(2)}) copy-start(f32[768]{0:T(1024)S(1)} %convert_element_type.199) | copy-start | bytes 9220
  60.9 32.7 %copy-start.30 = (f32[985]{0:T(1024)}, f32[985]{0:T(1024)S(1)}, u32[]{:S(2)}) copy-start(f32[985]{0:T(1024)S(1)} %add.154) | copy-start | bytes 11824
  60.9 32.7 %copy-start.36 = (f32[985]{0:T(1024)}, f32[985]{0:T(1024)S(1)}, u32[]{:S(2)}) copy-start(f32[985]{0:T(1024)S(1)} %rsqrt.20) | copy-start | bytes 11824
  135.2 4.8 copy-start.2
  135.2 4.8 copy-start.15
  155.8 1.6 copy-start.9
  298.8 10.6 %copy-start.10 = (f32[985,768]{1,0:T(8,128)S(1)}, f32[985,768]{1,0:T(8,128)}, u32[]{:S(2)}) copy-start(f32[985,768]{1,0:T(8,128)} %copy-done.9) | copy-start | bytes 9077764
  309.4 1.9 copy-start.11
  311.3 2.2 copy-start.22
  311.9 1.6 copy-start.8
  313.5 2.4 copy-start.45
  323.5 6.2 copy-start.16
  323.5 6.2 copy-start.23
  323.5 6.2 copy-start.29
  339.3 9.7 %copy-start.6 = (bf16[5,197,12,64]{1,3,2,0:T(8,128)(2,1)S(1)}, bf16[5,197,12,64]{1,3,2,0:T(8,128)(2,1)}, u32[]{:S(2)}) copy-start(bf16[5,197,12,64]{1,3,2,0:T(8,128)(2,1)} %copy.67) | copy-start | bytes 4538884
  346.5 2.6 copy-start.3
  349.1 2.7 copy-start.7
  351.7 145.4 %reduce-scatter.5.cloned.1.call-start = ((), (), s32[]{:S(2)}) async-start(), calls=%async_computation.8 | async-start | bytes 3981312 | tf_op jit(solution)/shard_map/reduce_scatter | solution.py:229
  351.8 6.4 copy-start.13
  361.3 5.7 copy-start.14
  370.2 5.7 copy-start.17
  386.7 5.9 copy-start.18
  392.6 1.4 copy-start.19
  392.6 1.9 copy-start.20
  394.0 2.7 copy-start.5
  394.0 2.7 copy-start.33
  394.0 2.7 copy-start.35
  394.0 2.7 copy-start.37
  394.0 2.7 copy-start.40
  394.0 2.7 copy-start.42
  394.6 2.1 copy-start.25
  403.2 192.7 %reduce-scatter.9.cloned.1.call-start = ((), (), s32[]{:S(2)}) async-start(), calls=%async_computation.10 | async-start | bytes 5308416 | tf_op jit(solution)/shard_map/reduce_scatter | solution.py:160
  413.6 281.0 %reduce-scatter.11.cloned.1.call-start = ((), (), s32[]{:S(2)}) async-start(), calls=%async_computation.11 | async-start | bytes 5308416 | tf_op jit(solution)/shard_map/reduce_scatter | solution.py:166
  423.5 0.7 copy-start.38
  423.5 2.1 copy-start.53
  423.5 2.6 copy-start.21
  423.5 2.6 copy-start.27
  423.6 462.0 %all-reduce.23.cloned.1.call-start = ((), (), s32[]{:S(2)}) async-start(), calls=%async_computation.12 | async-start | bytes 3538944 | tf_op jit(solution)/shard_map/psum | solution.py:257
  426.7 7.9 copy-start.31
  434.5 1.6 copy-start.12
  724.2 168.4 %copy-start.1 = (bf16[5,197,768]{2,1,0:T(8,128)(2,1)S(1)}, bf16[5,197,768]{2,1,0:T(8,128)(2,1)}, u32[]{:S(2)}) copy-start(bf16[5,197,768]{2,1,0:T(8,128)(2,1)} %param.16) | copy-start | bytes 4538884
  885.6 5.9 copy-start.24
Sparse Core Ops, SparseCore 0:
  10.2 66.8 all-gather.5
  79.3 39.5 all-gather.7
  121.1 78.8 all-gather.9
  202.1 78.0 all-gather.11
  351.9 61.5 reduce-scatter.6
  416.9 80.2 reduce-scatter.4
  500.8 95.0 reduce-scatter.8
  599.5 95.0 reduce-scatter.10
  697.2 46.5 all-reduce.22
where the time goes:
time: 915 us; the launch traced here: 900 us
  waiting for transfers between devices  315 us (34%)
  other arithmetic  198 us (22%)
  matrix products  161 us (18%)
  local copies, waits for them, and re-layouts  119 us (13%)
  blocking collectives  89.8 us (10%)
  between operations  17 us (2%)
    scatter-add x1, other arithmetic, shards(): grad_patches = jnp.zeros(patches.shape, jnp.float32).at[image_rows, slot_...  161 us
    reduce_scatter x1, waiting for transfers between devices, shards(): lax.psum_scatter(grad_up.astype(jnp.bfloat16), 'fsdp', scatter_dimension=...  98.7 us
    reduce_scatter x1, waiting for transfers between devices, shards(): lax.psum_scatter(grad_down.astype(jnp.bfloat16), 'fsdp', scatter_dimensio...  98.7 us
    unnamed x2, blocking collectives  61.3 us
    all_gather x1, waiting for transfers between devices, shards(): lax.all_gather(w_down, 'fsdp', axis=0, tiled=True)  43.4 us
    all_gather x1, waiting for transfers between devices, shards(): lax.all_gather(w_up, 'fsdp', axis=0, tiled=True)  41.5 us
    dot_general x4, matrix products, times_transpose(): lax.dot_general(left, right, (((1,), (1,)), ((), ())), preferred_element_...  40.3 us
    dot_general x1, matrix products, shards(): jnp.dot(normed_two_low, up_full, preferred_element_type=jnp.float32)  36.7 us
  transfers between devices with their start and end apart: 9, of which 5 were waited for; matrix products, arithmetic and copies ran while one was open for 43% of the time, Pallas kernels for 0%

commit v1 on v0

v1 whole, which is shorter than its diff:
```python
import functools
import math

import jax
import jax.numpy as jnp
from jax import lax
from jax.experimental import pallas as pl
from jax.experimental.pallas import tpu as pltpu
from jax.sharding import PartitionSpec as P

H = 12
HD = 64
EPSILON = 1e-06
F32 = jnp.float32
BF16 = jnp.bfloat16
SLOT = 200
ROWS = 1024
BLOCK = 128
TILE = 256
NT = (((1,), (1,)), ((), ()))


def dot(left, right):
    return jnp.dot(left, right, preferred_element_type=F32)


def dot_nt(left, right):
    return lax.dot_general(left, right, NT, preferred_element_type=F32)


def tile_at(index, size):
    return pl.ds(pl.multiple_of(index * size, size), size)


def norm_parts(values):
    centre = values - jnp.mean(values, axis=-1, keepdims=True)
    spread = jnp.mean(centre * centre, axis=-1, keepdims=True)
    inverse = lax.rsqrt(spread + EPSILON)
    return centre * inverse, inverse


def norm_back(hat, inverse, gain, grad):
    scaled = grad * gain
    along = jnp.mean(scaled * hat, axis=-1, keepdims=True)
    return inverse * (scaled - jnp.mean(scaled, axis=-1, keepdims=True) - hat * along)


def gelu_parts(hidden):
    size = jnp.abs(hidden)
    bell = jnp.exp(hidden * hidden * -0.5)
    t = 1.0 / (1.0 + size * (0.3275911 / math.sqrt(2.0)))
    tail = 1.061405429 * 0.5
    for term in (-1.453152027, 1.421413741, -0.284496736, 0.254829592):
        tail = tail * t + term * 0.5
    tail = tail * t * bell
    below = jnp.where(hidden >= 0, 1.0 - tail, tail)
    slope = below + hidden * (bell * (1.0 / math.sqrt(2.0 * math.pi)))
    return hidden * below, slope


def first_lanes(rows):
    return lax.broadcasted_iota(jnp.int32, (rows, 2 * HD), 1) < HD


def stage_gather(images, slots, patches, keep, stack, live, mask):
    stack[...] = jnp.zeros_like(stack)
    live[...] = jnp.zeros_like(live)

    def gather(i, _):
        row = keep[i]
        column = jnp.broadcast_to(row, (SLOT, SLOT)).T
        mask[i] = jnp.where(column >= 0, 0.0, -1e30)
        alive = (column >= 0).astype(F32)
        chosen = (column[:, :slots] == lax.broadcasted_iota(jnp.int32, (SLOT, slots), 1)).astype(F32).astype(BF16)
        rows = pl.ds(pl.multiple_of(i * SLOT, 8), SLOT)
        stack[rows, :] = dot(chosen, patches[i])
        live[rows, :] = alive[:, :BLOCK]
        return 0

    lax.fori_loop(0, images, gather, 0)


def stage_norm(stack, gain, shift, token, normed, normed_t):
    def norm(b, _):
        rows = tile_at(b, BLOCK)
        values = stack[rows, :]
        token[rows, :] = values.astype(BF16)
        hat, _ = norm_parts(values)
        low = (hat * gain + shift).astype(BF16)
        normed[rows, :] = low
        normed_t[:, rows] = low.T
        return 0

    lax.fori_loop(0, ROWS // BLOCK, norm, 0)


def stage_grads(images, slots, width, cot, stack, live, dm, dm_t):
    stack[...] = jnp.zeros_like(stack)
    for i in range(images):
        stack[i * SLOT : i * SLOT + slots, :] = cot[i].astype(F32)

    def grads(b, _):
        rows = tile_at(b, BLOCK)
        low = (stack[rows, :] * jnp.concatenate([live[rows, :]] * (width // BLOCK), axis=1)).astype(BF16)
        dm[rows, :] = low
        dm_t[:, rows] = low.T
        return 0

    lax.fori_loop(0, ROWS // BLOCK, grads, 0)


def stage_qkv(images, width, normed, w_qkv, bias, qkv):
    def body(c, _):
        cols = tile_at(c, TILE)
        scale = jnp.where(c < width // TILE, 1.0 / math.sqrt(HD), 1.0)
        values = (dot(normed[...], w_qkv[:, cols]) + bias[:, cols]) * scale
        for i in range(images):
            qkv[i, :, cols] = values[i * SLOT : (i + 1) * SLOT].astype(BF16)
        return 0

    lax.fori_loop(0, 3 * width // TILE, body, 0)


def stage_attention(images, width, qkv, mask, probs, stack, begin, end):
    pairs = H // 2

    def body(step, _):
        i, p = step // pairs, lax.rem(step, pairs)
        q2 = qkv[i, :, pl.ds(pl.multiple_of(p * 128, 128), 128)]
        k2 = qkv[i, :, pl.ds(pl.multiple_of(width + p * 128, 128), 128)]
        v2_t = qkv[i, :, pl.ds(pl.multiple_of(2 * width + p * 128, 128), 128)].T
        low = first_lanes(SLOT)
        outs = []
        for h in range(2):
            qh = jnp.where(low if h == 0 else ~low, q2, jnp.zeros_like(q2))
            scores = dot_nt(k2, qh) + mask[i]
            exponent = jnp.exp(scores - jnp.max(scores, axis=0, keepdims=True))
            share = 1.0 / jnp.sum(exponent, axis=0, keepdims=True)
            prob = (exponent * share).astype(BF16)
            probs[2 * step + h] = prob
            outs.append(dot(v2_t[h * HD : (h + 1) * HD], prob))
        stack[pl.ds(pl.multiple_of(i * SLOT, 8), SLOT), pl.ds(pl.multiple_of(p * 128, 128), 128)] = jnp.concatenate(outs, axis=0).T
        return 0

    lax.fori_loop(begin * pairs, end * pairs, body, 0)


def stage_out(width, stack, w_out, bias, token, gain, shift, att, att_t, middle, normed, normed_t):
    def low(b, _):
        rows = tile_at(b, BLOCK)
        values = stack[rows, :].astype(BF16)
        att[rows, :] = values
        att_t[:, rows] = values.T
        return 0

    lax.fori_loop(0, ROWS // BLOCK, low, 0)

    def body(c, _):
        cols = tile_at(c, TILE)
        middle[:, cols] = token[:, cols].astype(F32) + (dot(att[...], w_out[:, cols]) + bias[:, cols])
        return 0

    lax.fori_loop(0, width // TILE, body, 0)

    def norm(b, _):
        rows = tile_at(b, BLOCK)
        hat, _ = norm_parts(middle[rows, :])
        values = (hat * gain[...] + shift[...]).astype(BF16)
        normed[rows, :] = values
        normed_t[:, rows] = values.T
        return 0

    lax.fori_loop(0, ROWS // BLOCK, norm, 0)


def stage_mlp(width, hidden_width, normed, normed_t, dm, dm_t, w_up, b_up, w_down, act, dh, g_up, g_down_t, g_b_up):
    def body(c, _):
        cols = tile_at(c, TILE)
        hidden = dot(normed[...], w_up[:, cols]) + b_up[:, cols]
        d_act = dot_nt(dm[...], w_down[cols, :])
        value, slope = gelu_parts(hidden)
        value = value.astype(BF16)
        grad = (d_act * slope).astype(BF16)
        act[:, cols] = value
        dh[:, cols] = grad
        g_b_up[:, cols] = jnp.sum(grad.astype(F32), axis=0, keepdims=True)
        g_up[:, cols] = dot(normed_t[...], grad).astype(BF16)
        g_down_t[:, cols] = dot(dm_t[...], value).astype(BF16)
        return 0

    lax.fori_loop(0, hidden_width // TILE, body, 0)


def stage_mlp_out(images, slots, width, act, dh, w_up, w_down, b_down, middle, live, gain, dm, stack, out, d_mid_low, g_gain, g_shift, g_b_down, g_b_out):
    def body(c, _):
        cols = tile_at(c, TILE)
        stack[:, cols] = dot(act[...], w_down[:, cols])
        return 0

    lax.fori_loop(0, width // TILE, body, 0)

    def final(b, _):
        rows = tile_at(b, BLOCK)
        stack[rows, :] = (middle[rows, :] + (stack[rows, :] + b_down[...])) * jnp.concatenate([live[rows, :]] * (width // BLOCK), axis=1)
        return 0

    lax.fori_loop(0, ROWS // BLOCK, final, 0)
    for i in range(images):
        out[i] = stack[i * SLOT : i * SLOT + slots, :].astype(BF16)

    def body2(c, _):
        cols = tile_at(c, TILE)
        stack[:, cols] = dot_nt(dh[...], w_up[cols, :])
        return 0

    lax.fori_loop(0, width // TILE, body2, 0)
    for ref in (g_gain, g_shift, g_b_down, g_b_out):
        ref[...] = jnp.zeros_like(ref)

    def back(b, _):
        rows = tile_at(b, BLOCK)
        grad = stack[rows, :]
        hat, inverse = norm_parts(middle[rows, :])
        g_gain[...] += jnp.sum(grad * hat, axis=0, keepdims=True)
        g_shift[...] += jnp.sum(grad, axis=0, keepdims=True)
        own = dm[rows, :].astype(F32)
        g_b_down[...] += jnp.sum(own, axis=0, keepdims=True)
        total = own + norm_back(hat, inverse, gain[...], grad)
        middle[rows, :] = total
        low = total.astype(BF16)
        d_mid_low[rows, :] = low
        g_b_out[...] += jnp.sum(low.astype(F32), axis=0, keepdims=True)
        return 0

    lax.fori_loop(0, ROWS // BLOCK, back, 0)


def stage_out_back(width, att_t, d_mid_low, w_out, g_out, stack):
    def body(c, _):
        cols = tile_at(c, TILE)
        g_out[:, cols] = dot(att_t[...], d_mid_low[:, cols]).astype(BF16)
        stack[:, cols] = dot_nt(d_mid_low[...], w_out[cols, :])
        return 0

    lax.fori_loop(0, width // TILE, body, 0)


def stage_attention_back(images, width, qkv, probs, stack, d_qkv):
    pairs = H // 2

    def body(step, _):
        i, p = step // pairs, lax.rem(step, pairs)
        at_q = pl.ds(pl.multiple_of(p * 128, 128), 128)
        at_k = pl.ds(pl.multiple_of(width + p * 128, 128), 128)
        at_v = pl.ds(pl.multiple_of(2 * width + p * 128, 128), 128)
        q2, k2, v2 = qkv[i, :, at_q], qkv[i, :, at_k], qkv[i, :, at_v]
        k2_t = k2.T
        da = stack[pl.ds(pl.multiple_of(i * SLOT, 8), SLOT), at_q].astype(BF16)
        low = first_lanes(SLOT)
        dq, dk, dv = [], 0.0, 0.0
        for h in range(2):
            pick = lambda m: jnp.where(low if h == 0 else ~low, m, jnp.zeros_like(m))
            prob = probs[2 * step + h]
            d_prob = dot_nt(pick(v2), da)
            mixed = prob.astype(F32)
            moved = mixed * d_prob
            total = jnp.sum(moved, axis=0, keepdims=True)
            ds = (moved - mixed * total).astype(BF16)
            dq.append(dot(k2_t[h * HD : (h + 1) * HD], ds))
            dk = dk + dot(ds, pick(q2))
            dv = dv + dot(prob, pick(da))
        d_qkv[i, :, at_q] = (jnp.concatenate(dq, axis=0).T * (1.0 / math.sqrt(HD))).astype(BF16)
        d_qkv[i, :, at_k] = dk.astype(BF16)
        d_qkv[i, :, at_v] = dv.astype(BF16)
        return 0

    lax.fori_loop(0, images * pairs, body, 0)


def stage_qkv_back(images, width, d_qkv, normed_t, w_qkv, tile, flat, g_qkv, g_b_qkv, stack):
    tile[...] = jnp.zeros_like(tile)

    def body(c, _):
        cols = tile_at(c, TILE)
        for i in range(images):
            tile[i * SLOT : (i + 1) * SLOT, :] = d_qkv[i, :, cols].astype(F32)
        values = tile[...]
        g_b_qkv[:, cols] = jnp.sum(values, axis=0, keepdims=True)
        low = values.astype(BF16)
        flat[:, cols] = low
        g_qkv[:, cols] = dot(normed_t[...], low).astype(BF16)
        return 0

    lax.fori_loop(0, 3 * width // TILE, body, 0)

    def body2(c, _):
        cols = tile_at(c, TILE)
        stack[:, cols] = dot_nt(flat[:, : 3 * width], w_qkv[cols, :])
        return 0

    lax.fori_loop(0, width // TILE, body2, 0)


def stage_end(images, slots, width, keep, token, gain, middle, live, stack, g_gain, g_shift, grad_patches):
    for ref in (g_gain, g_shift):
        ref[...] = jnp.zeros_like(ref)

    def back(b, _):
        rows = tile_at(b, BLOCK)
        grad = stack[rows, :]
        hat, inverse = norm_parts(token[rows, :].astype(F32))
        g_gain[...] += jnp.sum(grad * hat, axis=0, keepdims=True)
        g_shift[...] += jnp.sum(grad, axis=0, keepdims=True)
        total = middle[rows, :] + norm_back(hat, inverse, gain[...], grad)
        stack[rows, :] = total * jnp.concatenate([live[rows, :]] * (width // BLOCK), axis=1)
        return 0

    lax.fori_loop(0, ROWS // BLOCK, back, 0)

    def scatter(i, _):
        chosen = (lax.broadcasted_iota(jnp.int32, (slots, SLOT), 0) == keep[i]).astype(F32).astype(BF16)
        values = stack[pl.ds(pl.multiple_of(i * SLOT, 8), SLOT), :]
        high = values.astype(BF16)
        rest = (values - high.astype(F32)).astype(BF16)
        grad_patches[i] = dot(chosen, high) + dot(chosen, rest)
        return 0

    lax.fori_loop(0, images, scatter, 0)


MESH = pl.DeviceIdType.MESH


class Place:
    def __init__(self):
        f, d = lax.axis_index("fsdp"), lax.axis_index("dp")
        self.z, self.x = f // 2, lax.rem(f, 2)
        self.y, self.c = d // 2, lax.rem(d, 2)
        z = self.z
        self.zs = [z, z + 1 - 2 * lax.rem(z, 2), lax.rem(z + 2, 4), 3 - z]

    def to(self, z=None, x=None, y=None, c=None):
        z, x, y, c = (own if new is None else new for new, own in ((z, self.z), (x, self.x), (y, self.y), (c, self.c)))
        return (z * 2 + x, y * 2 + c)

    def sides(self):
        return self.to(x=1 - self.x), self.to(y=1 - self.y), self.to(c=1 - self.c)


def enter(peers):
    barrier = pltpu.get_barrier_semaphore()
    for peer in peers:
        pl.semaphore_signal(barrier, inc=1, device_id=peer, device_id_type=MESH)
    pl.semaphore_wait(barrier, len(peers))


class Gather:
    def __init__(self, place, shard, full, first_cols, send, recv):
        self.place, self.shard, self.full, self.send, self.recv = place, shard, full, send, recv
        self.rows, cols = shard.shape
        self.half, self.wide, self.cut = self.rows // 2, cols // 2, first_cols
        self.started = []

    def spot(self, z, x, y, part=None, local=False):
        p = self.place
        base = 0 if local else (z * 2 + x) * self.rows
        rows = pl.ds(pl.multiple_of(base + p.c * self.half, 16), self.half)
        if y is None:
            return rows, slice(None)
        start, size = (y * self.wide, self.wide) if part is None else ((y * self.wide, self.cut) if part == 0 else (y * self.wide + self.cut, self.wide - self.cut))
        return rows, pl.ds(pl.multiple_of(start, 128), size)

    def copy(self, spot, sem, peer, local=None):
        src = self.full.at[spot] if local is None else self.shard.at[local]
        return pltpu.make_async_remote_copy(
            src_ref=src, dst_ref=self.full.at[spot], send_sem=self.send.at[sem], recv_sem=self.recv.at[sem], device_id=peer, device_id_type=MESH
        )

    def start(self, spot, sem, peer, local=None):
        copy = self.copy(spot, sem, peer, local)
        copy.start()
        self.started.append(copy)

    def arrived(self, spot, sem):
        self.copy(spot, sem, self.place.sides()[0]).wait_recv()

    def own(self, sem):
        p = self.place
        rows = pl.ds(pl.multiple_of((p.z * 2 + p.x) * self.rows, 16), self.rows)
        return pltpu.make_async_copy(self.shard, self.full.at[rows, :], sem)

    def begin(self):
        p = self.place
        side_x, side_y, _ = p.sides()
        spot, local = self.spot(p.z, p.x, p.y), self.spot(p.z, p.x, p.y, None, True)
        for k in (1, 2, 3):
            self.start(spot, k, p.to(z=p.zs[k]), local)
        self.start(spot, 4, side_x, local)
        self.start(self.spot(p.z, p.x, 1 - p.y, 1), 16, side_x, self.spot(p.z, p.x, 1 - p.y, 1, True))

    def spread(self, k):
        p = self.place
        side_x, side_y, _ = p.sides()
        spot = self.spot(p.zs[k], p.x, p.y)
        self.arrived(spot, k)
        self.start(spot, 4 + k, side_x)
        self.start(spot, 8 + k, side_y)

    def cross(self, k):
        p = self.place
        side_x, side_y, _ = p.sides()
        self.arrived(self.spot(p.zs[k], 1 - p.x, p.y), 4 + k)
        self.start(self.spot(p.zs[k], 1 - p.x, p.y, 0), 12 + k, side_y)
        if k:
            self.arrived(self.spot(p.zs[k], p.x, 1 - p.y), 8 + k)
            self.start(self.spot(p.zs[k], p.x, 1 - p.y, 1), 16 + k, side_x)

    def share(self, k):
        p = self.place
        core = p.sides()[2]
        if k:
            self.start(self.spot(p.zs[k], p.x, None), 20 + k, core)
        self.arrived(self.spot(p.zs[k], 1 - p.x, 1 - p.y, 0), 12 + k)
        self.arrived(self.spot(p.zs[k], 1 - p.x, 1 - p.y, 1), 16 + k)
        self.start(self.spot(p.zs[k], 1 - p.x, None), 24 + k, core)

    def finish(self):
        p = self.place

        def other(z, x):
            return pl.ds(pl.multiple_of((z * 2 + x) * self.rows + (1 - p.c) * self.half, 16), self.half), slice(None)

        for k in range(4):
            if k:
                self.arrived(other(p.zs[k], p.x), 20 + k)
            self.arrived(other(p.zs[k], 1 - p.x), 24 + k)

    def drain(self):
        for copy in self.started:
            copy.wait_send()
VMEM = pl.BlockSpec(memory_space=pltpu.VMEM)
ANY = pl.BlockSpec(memory_space=pl.ANY)
LIMIT = 61 * 1024 * 1024


def call(body, outs, scratch, args, name):
    return pl.pallas_call(
        body,
        out_shape=[jax.ShapeDtypeStruct(*o) for o in outs],
        in_specs=[VMEM] * len(args),
        out_specs=[VMEM] * len(outs),
        scratch_shapes=[pltpu.VMEM(*s) for s in scratch],
        compiler_params=pltpu.CompilerParams(vmem_limit_bytes=LIMIT),
        name=name,
    )(*args)


def first_plain(
    images, slots, width, patches, keep, cot, vectors, w_qkv, w_out,
    token, n1t, dm, dmt, live, qkv, probs, att_t, middle, n2, n2t, stack, normed, mask, att, bias,
):
    bias[...] = jnp.concatenate([vectors[2:3, :], jnp.zeros((1, width), F32), vectors[3:4, :]], axis=1)
    stage_gather(images, slots, patches, keep, stack, live, mask)
    stage_norm(stack, vectors[0:1, :], vectors[1:2, :], token, normed, n1t)
    stage_grads(images, slots, width, cot, stack, live, dm, dmt)
    stage_qkv(images, width, normed, w_qkv, bias, qkv)
    stage_attention(images, width, qkv, mask, probs, stack, 0, images)
    stage_out(width, stack, w_out, vectors.at[4:5, :], token, vectors.at[5:6, :], vectors.at[6:7, :], att, att_t, middle, n2, n2t)


def first_kernel(
    images, slots, width,
    patches, keep, cot, vec, s_qkv, s_out, s_up, s_down,
    token, n1t, dm, dmt, live, qkv, probs, att_t, middle, n2, n2t, vectors, b_up, o_qkv, o_out, f_up, f_down,
    stack, normed, mask, att, f_qkv, f_out, vecs, bias, q_send, q_recv, o_send, o_recv, u_send, u_recv, d_send, d_recv, v_send, v_recv, own,
):
    place = Place()
    side_x, side_y, side_c = place.sides()
    flat = [place.to(z=place.zs[k], x=x) for k in range(4) for x in (place.x, 1 - place.x)][1:]
    enter(flat + [side_y, side_c])
    g_qkv = Gather(place, s_qkv, f_qkv, 640, q_send, q_recv)
    g_out = Gather(place, s_out, f_out, 256, o_send, o_recv)
    g_up = Gather(place, s_up, f_up, 896, u_send, u_recv)
    g_down = Gather(place, s_down, f_down, 256, d_send, d_recv)
    mine = place.z * 2 + place.x
    tiny = []
    for j, peer in enumerate(flat):
        copy = pltpu.make_async_remote_copy(src_ref=vec, dst_ref=vecs.at[mine], send_sem=v_send.at[j], recv_sem=v_recv.at[j], device_id=peer, device_id_type=MESH)
        copy.start()
        tiny.append(copy)
    g_qkv.begin()
    locals_ = [g.own(own.at[j]) for j, g in enumerate((g_qkv, g_out, g_up, g_down))]
    for copy in locals_:
        copy.start()
    vecs[mine] = vec[...]
    stage_gather(images, slots, patches, keep, stack, live, mask)
    g_out.begin()
    for copy in tiny:
        copy.wait_recv()
    rows = jnp.concatenate([vecs[f][:, :96] for f in range(8)], axis=1).astype(F32)
    vectors[...] = rows
    b_up[...] = jnp.concatenate([vecs[f][8 + j : 9 + j, :96].astype(F32) for f in range(8) for j in range(4)], axis=1)
    for k in (1, 2, 3):
        g_qkv.spread(k)
    g_up.begin()
    stage_norm(stack, vectors[0:1, :], vectors[1:2, :], token, normed, n1t)
    for k in range(4):
        g_qkv.cross(k)
    for k in (1, 2, 3):
        g_out.spread(k)
    g_down.begin()
    stage_grads(images, slots, width, cot, stack, live, dm, dmt)
    for k in range(4):
        g_qkv.share(k)
    for k in range(4):
        g_out.cross(k)
    for k in (1, 2, 3):
        g_up.spread(k)
    locals_[0].wait()
    g_qkv.finish()
    keep_qkv = pltpu.make_async_copy(f_qkv, o_qkv, own.at[4])
    keep_qkv.start()
    bias[...] = jnp.concatenate([vectors[2:3, :], jnp.zeros((1, width), F32), vectors[3:4, :]], axis=1)
    stage_qkv(images, width, normed, f_qkv, bias, qkv)
    for k in range(4):
        g_out.share(k)
    for k in (1, 2, 3):
        g_down.spread(k)
    stage_attention(images, width, qkv, mask, probs, stack, 0, 1)
    for k in range(4):
        g_up.cross(k)
    stage_attention(images, width, qkv, mask, probs, stack, 1, 2)
    for k in range(4):
        g_up.share(k)
    stage_attention(images, width, qkv, mask, probs, stack, 2, 3)
    for k in range(4):
        g_down.cross(k)
    stage_attention(images, width, qkv, mask, probs, stack, 3, 4)
    stage_attention(images, width, qkv, mask, probs, stack, 4, images)
    locals_[1].wait()
    g_out.finish()
    keep_out = pltpu.make_async_copy(f_out, o_out, own.at[5])
    keep_out.start()
    stage_out(width, stack, f_out, vectors.at[4:5, :], token, vectors.at[5:6, :], vectors.at[6:7, :], att, att_t, middle, n2, n2t)
    for k in range(4):
        g_down.share(k)
    g_up.finish()
    g_down.finish()
    for copy in locals_[2:] + [keep_qkv, keep_out]:
        copy.wait()
    for copy in tiny:
        copy.wait_send()
    for g in (g_qkv, g_out, g_up, g_down):
        g.drain()


def shards(
    linked,
    patches, keep, ln1_gain, ln1_bias, w_qkv, b_query, b_value, w_out, b_out,
    ln2_gain, ln2_bias, w_up, b_up, w_down, b_down, cotangent,
):
    images, slots = keep.shape
    width = patches.shape[2]
    hidden_width = w_up.shape[1]
    keep_pad = jnp.pad(keep, ((0, 0), (0, SLOT - slots)), constant_values=-1).reshape(images, 1, SLOT)
    part = ln1_gain.shape[0]
    singles = [v.reshape(1, part) for v in (ln1_gain, ln1_bias, b_query, b_value, b_out, ln2_gain, ln2_bias, b_down)]
    rows_low, rows_wide = ((ROWS, width), BF16), ((ROWS, width), F32)
    cols_low = ((width, ROWS), BF16)
    live_like, mask_like = ((ROWS, BLOCK), F32), ((images, SLOT, SLOT), F32)
    heads_like = ((images, SLOT, 3 * width), BF16)
    probs_like = ((images * H, SLOT, SLOT), BF16)
    row_like = ((1, width), F32)

    if linked:
        vec = jnp.concatenate(singles + [b_up.reshape(4, part)], axis=0)
        vec = jnp.pad(vec, ((0, 4), (0, BLOCK - part)))
        full = lambda v: ((v.shape[0] * 8, v.shape[1]), BF16)
        outs = [
            rows_low, cols_low, rows_low, cols_low, live_like, heads_like, probs_like, cols_low, rows_wide, rows_low, cols_low,
            ((16, width), F32), ((1, hidden_width), F32), full(w_qkv), full(w_out), full(w_up), full(w_down),
        ]
        scratch = [rows_wide, rows_low, mask_like, rows_low, full(w_qkv), full(w_out), ((8, 16, BLOCK), BF16), ((1, 3 * width), F32)]
        token, n1t, dm, dmt, live, qkv, probs, att_t, middle, n2, n2t, vectors, bias_up, qkv_full, out_full, up_full, down_full = pl.pallas_call(
            functools.partial(first_kernel, images, slots, width),
            out_shape=[jax.ShapeDtypeStruct(*o) for o in outs],
            in_specs=[VMEM] * 8,
            out_specs=[VMEM] * 13 + [ANY] * 4,
            scratch_shapes=[pltpu.VMEM(*s) for s in scratch]
            + [pltpu.SemaphoreType.DMA((28,))] * 8
            + [pltpu.SemaphoreType.DMA((7,))] * 2
            + [pltpu.SemaphoreType.DMA((6,))],
            compiler_params=pltpu.CompilerParams(vmem_limit_bytes=LIMIT, collective_id=0, has_side_effects=True),
            name="first",
        )(patches, keep_pad, cotangent, vec, w_qkv, w_out, w_up, w_down)
    else:
        gather = lambda v: lax.all_gather(v, "fsdp", axis=0, tiled=True)
        vectors = jnp.pad(gather(jnp.concatenate(singles, axis=0).T).T.astype(F32), ((0, 8), (0, 0)))
        bias_up = gather(b_up).astype(F32).reshape(1, hidden_width)
        qkv_full, out_full, up_full, down_full = gather(w_qkv), gather(w_out), gather(w_up), gather(w_down)
        outs = [rows_low, cols_low, rows_low, cols_low, live_like, heads_like, probs_like, cols_low, rows_wide, rows_low, cols_low]
        scratch = [rows_wide, rows_low, mask_like, rows_low, ((1, 3 * width), F32)]
        token, n1t, dm, dmt, live, qkv, probs, att_t, middle, n2, n2t = call(
            functools.partial(first_plain, images, slots, width),
            outs, scratch, (patches, keep_pad, cotangent, vectors, qkv_full, out_full), "first",
        )
    gain1, gain2, b_d = vectors[0:1], vectors[5:6], vectors[7:8]

    def second(n2, n2t, dm, dmt, w_up, b_up, w_down, b_d, middle_in, live, gain2, out, middle, d_low, g_up, g_down_t, g_b_up, g_g2, g_s2, g_bd, g_bo, act, dh, stack):
        middle[...] = middle_in[...]
        stage_mlp(width, hidden_width, n2, n2t, dm, dmt, w_up, b_up, w_down, act, dh, g_up, g_down_t, g_b_up)
        stage_mlp_out(images, slots, width, act, dh, w_up, w_down, b_d, middle, live, gain2, dm, stack, out, d_low, g_g2, g_s2, g_bd, g_bo)

    hid = ((ROWS, hidden_width), BF16)
    out_tokens, d_mid, d_low, g_up, g_down_t, g_b_up, g_g2, g_s2, g_bd, g_bo = call(
        second,
        [((images, slots, width), BF16), rows_wide, rows_low, ((width, hidden_width), BF16), ((width, hidden_width), BF16), ((1, hidden_width), F32)] + [row_like] * 4,
        [hid, hid, rows_wide],
        (n2, n2t, dm, dmt, up_full, bias_up, down_full, b_d, middle, live, gain2),
        "second",
    )

    def third(d_low, att_t, w_out, qkv, probs, n1t, w_qkv, token, gain1, d_mid, live, keep, g_out, g_qkv, g_b, g_g1, g_s1, gp, stack, tile, flat, d_qkv):
        stage_out_back(width, att_t, d_low, w_out, g_out, stack)
        stage_attention_back(images, width, qkv, probs, stack, d_qkv)
        stage_qkv_back(images, width, d_qkv, n1t, w_qkv, tile, flat, g_qkv, g_b, stack)
        stage_end(images, slots, width, keep, token, gain1, d_mid, live, stack, g_g1, g_s1, gp)

    g_out, g_qkv, g_b, g_g1, g_s1, grad_patches = call(
        third,
        [((width, width), BF16), ((width, 3 * width), BF16), ((1, 3 * width), F32), row_like, row_like, ((images, slots, width), F32)],
        [rows_wide, ((ROWS, TILE), F32), ((ROWS, 3 * width), BF16), heads_like],
        (d_low, att_t, out_full, qkv, probs, n1t, qkv_full, token, gain1, d_mid, live, keep_pad),
        "third",
    )
    both = ("fsdp", "dp")
    scat = lambda v, dim=0: lax.psum(lax.psum_scatter(v, "fsdp", scatter_dimension=dim, tiled=True), "dp").astype(F32)
    small = jnp.concatenate([g_g1, g_s1, g_b[:, :width], g_b[:, 2 * width :], g_bo, g_g2, g_s2, g_bd], axis=0).astype(BF16)
    small = scat(small, 1)
    b_up_sum = scat(g_b_up.astype(BF16), 1)[0]
    return (
        out_tokens, grad_patches, small[0], small[1], scat(g_qkv), small[2], small[3], scat(g_out), small[4],
        small[5], small[6], scat(g_up), b_up_sum, scat(g_down_t, 1).T, small[7],
    )


def solution(mesh):
    linked = (mesh.shape["fsdp"], mesh.shape["dp"]) == (8, 4)
    many, one, two = P(("fsdp", "dp"), None, None), P("fsdp"), P("fsdp", None)
    in_specs = (many, P(("fsdp", "dp"), None), one, one, two, one, one, two, one, one, one, two, one, two, one, many)
    out_specs = (many, many, one, one, two, one, one, two, one, one, one, two, one, two, one)
    return jax.shard_map(functools.partial(shards, linked), mesh=mesh, in_specs=in_specs, out_specs=out_specs, check_vma=False)
```

time: 915 us -> 711 us (0.78); the launches traced: 900 us -> 710 us
  Pallas kernels: 0 us -> 209 us
  other arithmetic: 198 us -> 4.41 us
  matrix products: 161 us -> 0 us
  waiting for transfers between devices: 315 us -> 453 us
  local copies, waits for them, and re-layouts: 119 us -> 20.7 us
  blocking collectives: 89.8 us -> 7.55 us
    pallas_call x0 -> x3, Pallas kernels: none -> 209 us  [the longest x2 111 us: call(): pl.pallas_call(body, out_shape=[jax.ShapeDtypeStruct(*o) for o in outs],...]
    unnamed x9 -> x10, waiting for transfers between devices: 2.66 us -> 166 us
    scatter-add x1 -> x0, other arithmetic: 161 us -> none  [shards(): grad_patches = jnp.zeros(patches.shape, jnp.float32).at[image_rows, slot_...]
    dot_general x18 -> x0, matrix products: 161 us -> none  [the longest x4 40.3 us: times_transpose(): lax.dot_general(left, right, (((1,), (1,)), ((), ())), preferred_element_...]
    all_gather x4 -> x0, waiting for transfers between devices: 84.9 us -> none  [the longest x1 43.4 us: shards(): lax.all_gather(w_down, 'fsdp', axis=0, tiled=True)]
    reshape x14 -> x2, local copies, waits for them, and re-layouts: 72.7 us -> 1.36 us  [the longest x1 0.76 us: shards(): vec = jnp.concatenate(singles + [b_up.reshape(4, part)], axis=0)]
    unnamed x2 -> x0, blocking collectives: 61.3 us -> none
    psum x1, waiting for transfers between devices: 0.01 us -> 41.4 us  [shards(): lax.psum(lax.psum_scatter(v, 'fsdp', scatter_dimension=dim, tiled=True),...]
  transfers between devices with their start and end apart: 9 -> 7, of which waited for: 5 -> 7; matrix products, arithmetic and copies ran while one was open for 43% -> 1% of each run, Pallas kernels for 0% -> 8%
where the time goes in v1:
time: 711 us; the launch traced here: 710 us
  waiting for transfers between devices  453 us (64%)
  Pallas kernels  209 us (29%)
  local copies, waits for them, and re-layouts  20.7 us (3%)
  between operations  14.3 us (2%)
  blocking collectives  7.55 us (1%)
    reduce_scatter x3, waiting for transfers between devices, shards(): lax.psum_scatter(v, 'fsdp', scatter_dimension=dim, tiled=True)  246 us
    unnamed x10, waiting for transfers between devices  166 us
    pallas_call x2, Pallas kernels, call(): pl.pallas_call(body, out_shape=[jax.ShapeDtypeStruct(*o) for o in outs],...  111 us
    pallas_call x1, Pallas kernels, shards(): pl.pallas_call(functools.partial(first_kernel, images, slots, width), out...  98.1 us
    psum x1, waiting for transfers between devices, shards(): lax.psum(lax.psum_scatter(v, 'fsdp', scatter_dimension=dim, tiled=True),...  41.4 us
  transfers between devices with their start and end apart: 7, of which 7 were waited for; matrix products, arithmetic and copies ran while one was open for 1% of the time, Pallas kernels for 8%

profile of v1, /device:TPU:1, one launch (start us, length us, event | category | flops | bytes accessed | tf_op | source)
XLA Modules:
  0.0 709.9 jit_solution(18167792845156677661)
XLA Ops:
  7.2 0.0 reduce-scatter.23.cloned.1.call-start
  7.2 0.8 reshape.69
  8.0 0.7 pad.8
  8.7 0.6 reshape.60.keep
  9.3 0.8 concatenate.7
  10.1 0.6 pad.9.vec
  10.7 98.1 %first.1 = (bf16[1024,768]{1,0:T(8,128)(2,1)}, bf16[768,1024]{1,0:T(8,128)(2,1)}, bf16[1024,768]{1,0:T(8,128)(2,1)}, bf16[768,1024]{1,0:T(8,128)(2,1)}, f32[1024...) custom-call(bf16[5,197,768]{2,1,0:T(8,128)(2,1)} %patches.1, ...), custom_call_target="tpu_custom_call" | custom-call | tf_op jit(solution)/shard_map/first/pallas_call | solution.py:584
  108.9 1.5 fusion
  110.3 57.5 %second.1 = (bf16[5,197,768]{2,1,0:T(8,128)(2,1)}, f32[1024,768]{1,0:T(8,128)}, bf16[1024,768]{1,0:T(8,128)(2,1)}, bf16[768,3072]{1,0:T(8,128)(2,1)}, bf16[768,3...) custom-call(bf16[1024,768]{1,0:T(8,128)(2,1)} %get-tuple-element.48., ...), custom_call_target="tpu_custom_call" | custom-call | tf_op jit(solution)/shard_map/second/pallas_call | solution.py:447
  167.8 6.7 copy.37
  174.5 0.0 reduce-scatter.23.cloned.1.call-update
  174.5 0.0 reduce-scatter.15.cloned.1.call-start
  174.6 53.6 %third.1 = (bf16[768,768]{1,0:T(8,128)(2,1)}, bf16[768,2304]{1,0:T(8,128)(2,1)}, f32[1,2304]{1,0:T(1,128)}, f32[1,768]{1,0:T(1,128)}, f32[1,768]{1,0:T(1,128)}, /*index=5*/f32[5,197,768]{2,1,0:T(8,128)}) custom-call(bf16[1024,768]{1,0:T(8,128)(2,1)} %get-tuple-element.59.d_low, bf16[768,1024]{1,0:T(8,128)(2,1)} %get-tuple-element.60.att_t, ...), custom_call_target="tpu_custom_call" | custom-call | tf_op jit(solution)/shard_map/third/pallas_call | solution.py:447
  228.1 0.0 reduce-scatter.15.cloned.1.call-update
  228.1 0.0 reduce-scatter.13.cloned.1.call-start
  228.2 0.7 reduce-scatter.13.cloned.1.call-update
  228.9 0.0 reduce-scatter.17.cloned.1.call-start
  228.9 0.0 copy-start.2
  228.9 0.5 reduce-scatter.17.cloned.1.call-update
  229.5 0.0 copy-start.3
  229.5 0.0 copy-start.9
  229.5 0.0 copy-start.8
  229.5 0.0 copy-start.7
  229.5 0.0 copy-start.6
  229.5 0.0 copy-start.5
  229.5 0.0 copy-start.4
  229.5 0.0 reduce-scatter.21.cloned.1.call-start
  229.6 0.1 copy-done.2
  229.7 1.2 copy.35
  230.9 0.0 reduce-scatter.21.cloned.1.call-update
  230.9 0.0 reduce-scatter.19.cloned.1.call-start
  231.0 0.0 copy-done.3
  231.0 0.0 copy-done.9
  231.0 0.0 copy-done.8
  231.0 0.0 copy-done.7
  231.1 0.0 copy-done.6
  231.1 0.0 copy-done.5
  231.1 0.0 copy-done.4
  231.1 0.1 concatenate.8
  231.2 0.8 copy.33
  232.0 0.0 reduce-scatter.19.cloned.1.call-update
  232.0 0.0 all-reduce.6.cloned.1.call-start
  232.1 37.6 %reduce-scatter.23.cloned.1.call-done = bf16[384,768]{1,0:T(8,128)(2,1)} async-done(((bf16[3072,768]{1,0:T(8,128)(2,1)}), bf16[384,768]{1,0:T(8,128)(2,1)}) %reduce-scatter.23.cloned.1.call-update) | async-done | bytes 589840
  269.7 2.1 copy.38
  271.8 64.1 %reduce-scatter.15.cloned.1.call-done = bf16[96,768]{1,0:T(8,128)(2,1)} async-done(((bf16[768,768]{1,0:T(8,128)(2,1)}), bf16[96,768]{1,0:T(8,128)(2,1)}) %reduce-scatter.15.cloned.1.call-update) | async-done | bytes 147472 | tf_op jit(solution)/shard_map/reduce_scatter | solution.py:637
  335.9 83.1 %reduce-scatter.13.cloned.1.call-done = bf16[96,2304]{1,0:T(8,128)(2,1)} async-done(((bf16[768,2304]{1,0:T(8,128)(2,1)}), bf16[96,2304]{1,0:T(8,128)(2,1)}) %reduce-scatter.13.cloned.1.call-update) | async-done | bytes 442384 | tf_op jit(solution)/shard_map/reduce_scatter | solution.py:637
  419.0 98.7 %reduce-scatter.17.cloned.1.call-done = bf16[96,3072]{1,0:T(8,128)(2,1)} async-done(((bf16[768,3072]{1,0:T(8,128)(2,1)}), bf16[96,3072]{1,0:T(8,128)(2,1)}) %reduce-scatter.17.cloned.1.call-update) | async-done | bytes 589840 | tf_op jit(solution)/shard_map/reduce_scatter | solution.py:637
  517.8 0.0 all-reduce.6.cloned.1.call-update
  517.8 64.2 %reduce-scatter.21.cloned.1.call-done = bf16[384,1]{1,0:T(8,128)(2,1)} async-done(((bf16[3072,1]{1,0:T(8,128)(2,1)}), bf16[384,1]{1,0:T(8,128)(2,1)}) %reduce-scatter.21.cloned.1.call-update) | async-done | bytes 784
  582.1 1.0 bitcast_reduce_fusion
  583.1 63.0 %reduce-scatter.19.cloned.1.call-done = bf16[96,8]{1,0:T(8,128)(2,1)} async-done(((bf16[768,8]{1,0:T(8,128)(2,1)}), bf16[96,8]{1,0:T(8,128)(2,1)}) %reduce-scatter.19.cloned.1.call-update) | async-done | bytes 1552
  646.1 0.8 copy.34
  646.9 7.5 %all-reduce.2 = (bf16[8,96]{1,0:T(8,128)(2,1)S(1)}, bf16[384]{0:T(512)(128)(2,1)S(1)}) all-reduce(bf16[8,96]{1,0:T(8,128)(2,1)S(1)} %copy.34, bf16[384]{0:T(512)(128)(2,1)S(1)} %bitcast_reduce_fusion), channel_id=1, replica_groups=mesh['fsdp'=8,'dp'=4] {'dp'}, use_global_device_ids=true, to_apply=%region_1.2 | all-reduce | flops 1152 | bytes 4608 | tf_op jit(solution)/shard_map/psum | solution.py:637
  654.4 0.6 squeeze.38
  655.0 0.5 slice_bitcast_fusion
  655.5 41.4 %all-reduce.6.cloned.1.call-done = (bf16[384,768]{0,1:T(8,128)(2,1)}, bf16[96,2304]{1,0:T(8,128)(2,1)}, bf16[96,768]{1,0:T(8,128)(2,1)}, bf16[96,3072]{1,0:T(8,128)(2,1)}) async-done(((bf16[384,768]{0,1:T(8,128)(2,1)}, bf16[96,2304]{1,0:T(8,128)(2,1)}, bf16[96,768]{1,0:T(8,128)(2,1)}, bf16[96,3072]{1,0:T(8,128)(2,1)}), (bf16[384,768]{0,1:T(8,128)(2,1)}, bf16[96,2304]{1,0:T(8,128)(2,1)}, ...) | async-done | bytes 1769488 | tf_op jit(solution)/shard_map/psum | solution.py:637
  696.9 0.0 copy-start.1
  696.9 1.7 convert_element_type.22
  698.6 0.0 copy-start
  698.6 2.4 copy.32
  701.0 0.0 copy-done.1
  701.0 1.0 convert_element_type.21
  701.9 0.0 copy-done
  702.0 1.1 convert_element_type.23
  (10 shorter events, 0.1 us)
Async XLA Ops:
  7.2 262.5 %reduce-scatter.23.cloned.1.call-start = ((), (), s32[]{:S(2)}) async-start(), calls=%async_computation.11 | async-start | bytes 5308416
  174.5 161.4 %reduce-scatter.15.cloned.1.call-start = ((), (), s32[]{:S(2)}) async-start(), calls=%async_computation.7 | async-start | bytes 1327104 | tf_op jit(solution)/shard_map/reduce_scatter | solution.py:637
  228.1 190.9 %reduce-scatter.13.cloned.1.call-start = ((), (), s32[]{:S(2)}) async-start(), calls=%async_computation.6 | async-start | bytes 3981312 | tf_op jit(solution)/shard_map/reduce_scatter | solution.py:637
  228.9 288.9 %reduce-scatter.17.cloned.1.call-start = ((), (), s32[]{:S(2)}) async-start(), calls=%async_computation.8 | async-start | bytes 5308416 | tf_op jit(solution)/shard_map/reduce_scatter | solution.py:637
  228.9 0.7 copy-start.2
  229.5 1.5 copy-start.3
  229.5 1.5 copy-start.9
  229.5 1.5 copy-start.8
  229.5 1.5 copy-start.7
  229.5 1.6 copy-start.6
  229.5 1.6 copy-start.5
  229.5 1.6 copy-start.4
  229.5 352.5 %reduce-scatter.21.cloned.1.call-start = ((), (), s32[]{:S(2)}) async-start(), calls=%async_computation.10 | async-start | bytes 884736
  230.9 415.2 %reduce-scatter.19.cloned.1.call-start = ((), (), s32[]{:S(2)}) async-start(), calls=%async_computation.9 | async-start | bytes 221184
  232.0 464.9 %all-reduce.6.cloned.1.call-start = ((), (), s32[]{:S(2)}) async-start(), calls=%async_computation.12 | async-start | bytes 3538944 | tf_op jit(solution)/shard_map/psum | solution.py:637
  696.9 4.1 copy-start.1
  698.6 3.4 copy-start
Sparse Core Ops, SparseCore 0:
  174.6 94.9 reduce-scatter.22
  273.6 62.2 reduce-scatter.14
  339.5 79.4 reduce-scatter.12
  422.5 95.2 reduce-scatter.16
  521.5 60.4 reduce-scatter.20
  586.1 59.9 reduce-scatter.18
  649.4 47.4 all-reduce.5

commit v2 on v1

--- a/solution.py
+++ b/solution.py
@@ -173,7 +173,7 @@
     lax.fori_loop(0, ROWS // BLOCK, norm, 0)
 
 
-def stage_mlp(width, hidden_width, normed, normed_t, dm, dm_t, w_up, b_up, w_down, act, dh, g_up, g_down_t, g_b_up):
+def stage_mlp(width, hidden_width, normed, normed_t, dm, dm_t, w_up, b_up, w_down, act, dh, put_up, put_down, g_b_up):
     def body(c, _):
         cols = tile_at(c, TILE)
         hidden = dot(normed[...], w_up[:, cols]) + b_up[:, cols]
@@ -184,8 +184,8 @@
         act[:, cols] = value
         dh[:, cols] = grad
         g_b_up[:, cols] = jnp.sum(grad.astype(F32), axis=0, keepdims=True)
-        g_up[:, cols] = dot(normed_t[...], grad).astype(BF16)
-        g_down_t[:, cols] = dot(dm_t[...], value).astype(BF16)
+        put_up(c, dot(normed_t[...], grad).astype(BF16))
+        put_down(c, dot(dm_t[...], value).astype(BF16))
         return 0
 
     lax.fori_loop(0, hidden_width // TILE, body, 0)
@@ -235,21 +235,18 @@
     lax.fori_loop(0, ROWS // BLOCK, back, 0)
 
 
-def stage_out_back(width, att_t, d_mid_low, w_out, g_out, stack):
+def stage_out_back(width, att_t, d_mid_low, w_out, put_out, stack):
     def body(c, _):
         cols = tile_at(c, TILE)
-        g_out[:, cols] = dot(att_t[...], d_mid_low[:, cols]).astype(BF16)
+        put_out(c, dot(att_t[...], d_mid_low[:, cols]).astype(BF16))
         stack[:, cols] = dot_nt(d_mid_low[...], w_out[cols, :])
         return 0
 
     lax.fori_loop(0, width // TILE, body, 0)
 
 
-def stage_attention_back(images, width, qkv, probs, stack, d_qkv):
-    pairs = H // 2
-
-    def body(step, _):
-        i, p = step // pairs, lax.rem(step, pairs)
+def stage_attention_back(width, qkv, probs, stack, i, begin, end):
+    def body(p, _):
         at_q = pl.ds(pl.multiple_of(p * 128, 128), 128)
         at_k = pl.ds(pl.multiple_of(width + p * 128, 128), 128)
         at_v = pl.ds(pl.multiple_of(2 * width + p * 128, 128), 128)
@@ -260,7 +257,7 @@
         dq, dk, dv = [], 0.0, 0.0
         for h in range(2):
             pick = lambda m: jnp.where(low if h == 0 else ~low, m, jnp.zeros_like(m))
-            prob = probs[2 * step + h]
+            prob = probs[2 * p + h]
             d_prob = dot_nt(pick(v2), da)
             mixed = prob.astype(F32)
             moved = mixed * d_prob
@@ -269,17 +266,15 @@
             dq.append(dot(k2_t[h * HD : (h + 1) * HD], ds))
             dk = dk + dot(ds, pick(q2))
             dv = dv + dot(prob, pick(da))
-        d_qkv[i, :, at_q] = (jnp.concatenate(dq, axis=0).T * (1.0 / math.sqrt(HD))).astype(BF16)
-        d_qkv[i, :, at_k] = dk.astype(BF16)
-        d_qkv[i, :, at_v] = dv.astype(BF16)
-        return 0
-
-    lax.fori_loop(0, images * pairs, body, 0)
-
-
-def stage_qkv_back(images, width, d_qkv, normed_t, w_qkv, tile, flat, g_qkv, g_b_qkv, stack):
-    tile[...] = jnp.zeros_like(tile)
-
+        qkv[i, :, at_q] = (jnp.concatenate(dq, axis=0).T * (1.0 / math.sqrt(HD))).astype(BF16)
+        qkv[i, :, at_k] = dk.astype(BF16)
+        qkv[i, :, at_v] = dv.astype(BF16)
+        return 0
+
+    lax.fori_loop(begin, end, body, 0)
+
+
+def stage_qkv_back(images, width, d_qkv, normed_t, tile, flat, put_qkv, g_b_qkv, begin, end):
     def body(c, _):
         cols = tile_at(c, TILE)
         for i in range(images):
@@ -288,20 +283,22 @@
         g_b_qkv[:, cols] = jnp.sum(values, axis=0, keepdims=True)
         low = values.astype(BF16)
         flat[:, cols] = low
-        g_qkv[:, cols] = dot(normed_t[...], low).astype(BF16)
-        return 0
-
-    lax.fori_loop(0, 3 * width // TILE, body, 0)
-
-    def body2(c, _):
+        put_qkv(c, dot(normed_t[...], low).astype(BF16))
+        return 0
+
+    lax.fori_loop(begin, end, body, 0)
+
+
+def stage_norm_back(width, flat, w_qkv, stack):
+    def body(c, _):
         cols = tile_at(c, TILE)
-        stack[:, cols] = dot_nt(flat[:, : 3 * width], w_qkv[cols, :])
-        return 0
-
-    lax.fori_loop(0, width // TILE, body2, 0)
-
-
-def stage_end(images, slots, width, keep, token, gain, middle, live, stack, g_gain, g_shift, grad_patches):
+        stack[:, cols] = dot_nt(flat[...], w_qkv[cols, :])
+        return 0
+
+    lax.fori_loop(0, width // TILE, body, 0)
+
+
+def stage_end(images, slots, width, keep, token, gain, middle, live, stack, g_gain, g_shift, put_patches):
     for ref in (g_gain, g_shift):
         ref[...] = jnp.zeros_like(ref)
 
@@ -322,10 +319,11 @@
         values = stack[pl.ds(pl.multiple_of(i * SLOT, 8), SLOT), :]
         high = values.astype(BF16)
         rest = (values - high.astype(F32)).astype(BF16)
-        grad_patches[i] = dot(chosen, high) + dot(chosen, rest)
-        return 0
-
-    lax.fori_loop(0, images, scatter, 0)
+        put_patches(i, dot(chosen, high) + dot(chosen, rest))
+        return 0
+
+    for i in range(images):
+        scatter(i, 0)
 
 
 MESH = pl.DeviceIdType.MESH
@@ -438,6 +436,156 @@
     def drain(self):
         for copy in self.started:
             copy.wait_send()
+
+
+class Reduce:
+    def __init__(self, place, source, held, core, diag_x, diag_y, side_x, side_y, line, final, send, recv):
+        self.place, self.source, self.held, self.core = place, source, held, core
+        self.diag_x, self.diag_y, self.side_x, self.side_y, self.line, self.final = diag_x, diag_y, side_x, side_y, line, final
+        self.send, self.recv, self.started = send, recv, []
+        self.by_rows = diag_y.shape[2] == final.shape[3]
+        self.cut = diag_y.shape[1] if self.by_rows else diag_y.shape[2]
+
+    def part(self, second):
+        bounds = pl.ds(self.cut, (self.final.shape[2] if self.by_rows else self.final.shape[3]) - self.cut) if second else pl.ds(0, self.cut)
+        return (bounds, slice(None)) if self.by_rows else (slice(None), bounds)
+
+    def hold(self, z, x, y, *rest):
+        if self.held is None:
+            return (z, x, self.place.c, y) + rest
+        return (z, x, y) + rest
+
+    @property
+    def home(self):
+        return self.source if self.held is None else self.held
+
+    def copy(self, src, dst, sem, peer):
+        return pltpu.make_async_remote_copy(src_ref=src, dst_ref=dst, send_sem=self.send.at[sem], recv_sem=self.recv.at[sem], device_id=peer, device_id_type=MESH)
+
+    def start(self, src, dst, sem, peer):
+        copy = self.copy(src, dst, sem, peer)
+        copy.start()
+        self.started.append(copy)
+
+    def arrived(self, dst, sem):
+        self.copy(dst, dst, sem, self.place.sides()[0]).wait_recv()
+
+    def begin(self, own=None):
+        p = self.place
+        self.start(self.source.at[:, :, 1 - p.c], self.core, 0, p.sides()[2])
+        self.own = own
+        if own is not None:
+            own.start()
+
+    def add_core(self, x, y):
+        def body(z, _):
+            spot = self.hold(z, x, y)
+            self.home[spot] = self.home[spot] + self.core[z, x, y]
+            return 0
+
+        lax.fori_loop(0, 4, body, 0)
+
+    def add(self, x, y, part, buffer):
+        def body(z, _):
+            spot = self.hold(z, x, y, *part)
+            self.home[spot] = self.home[spot] + buffer[z]
+            return 0
+
+        lax.fori_loop(0, 4, body, 0)
+
+    def step_core(self):
+        p = self.place
+        side_x, side_y, _ = p.sides()
+        if self.own is not None:
+            self.own.wait()
+        self.arrived(self.core, 0)
+        self.add_core(1 - p.x, 1 - p.y)
+        every = slice(None)
+        self.start(self.home.at[self.hold(every, 1 - p.x, 1 - p.y, *self.part(True))], self.diag_x, 1, side_x)
+        self.start(self.home.at[self.hold(every, 1 - p.x, 1 - p.y, *self.part(False))], self.diag_y, 2, side_y)
+        self.add_core(1 - p.x, p.y)
+        self.add_core(p.x, 1 - p.y)
+        self.add_core(p.x, p.y)
+
+    def step_diag(self):
+        p = self.place
+        side_x, side_y, _ = p.sides()
+        every = slice(None)
+        self.arrived(self.diag_y, 2)
+        self.add(1 - p.x, p.y, self.part(False), self.diag_y)
+        self.start(self.home.at[self.hold(every, 1 - p.x, p.y)], self.side_x, 3, side_x)
+        self.arrived(self.diag_x, 1)
+        self.add(p.x, 1 - p.y, self.part(True), self.diag_x)
+        self.start(self.home.at[self.hold(every, p.x, 1 - p.y)], self.side_y, 4, side_y)
+
+    def step_side(self):
+        p = self.place
+        whole = (slice(None), slice(None))
+        self.arrived(self.side_x, 3)
+        self.add(p.x, p.y, whole, self.side_x)
+        self.arrived(self.side_y, 4)
+        self.add(p.x, p.y, whole, self.side_y)
+        for k in (1, 2, 3):
+            self.start(self.home.at[self.hold(p.zs[k], p.x, p.y)], self.line.at[k - 1], 4 + k, p.to(z=p.zs[k]))
+
+    def step_line(self):
+        p = self.place
+        total = self.home[self.hold(p.z, p.x, p.y)].astype(F32)
+        for k in (1, 2, 3):
+            self.arrived(self.line.at[k - 1], 4 + k)
+            total = total + self.line[k - 1].astype(F32)
+        self.final[p.c, p.y] = total.astype(BF16)
+        self.start(self.final.at[p.c, p.y], self.final.at[p.c, p.y], 8, p.sides()[1])
+
+    def step_share(self):
+        p = self.place
+        self.arrived(self.final.at[p.c, 1 - p.y], 8)
+        self.start(self.final.at[p.c], self.final.at[p.c], 9, p.sides()[2])
+
+    def finish(self):
+        self.arrived(self.final.at[1 - self.place.c], 9)
+
+    def drain(self):
+        for copy in self.started:
+            copy.wait_send()
+
+
+class SmallReduce:
+    def __init__(self, place, home, core, side_y, side_x, line, send, recv):
+        self.place, self.home, self.core, self.side_y, self.side_x, self.line = place, home, core, side_y, side_x, line
+        self.send, self.recv, self.started = send, recv, []
+
+    copy, start, arrived, drain = Reduce.copy, Reduce.start, Reduce.arrived, Reduce.drain
+
+    def begin(self):
+        self.start(self.home, self.core, 0, self.place.sides()[2])
+
+    def step_core(self, sent):
+        p = self.place
+        self.arrived(self.core, 0)
+        sent[...] = self.home[...] + self.core[...]
+        self.start(sent, self.side_y, 1, p.sides()[1])
+
+    def step_y(self, sent, total):
+        p = self.place
+        self.arrived(self.side_y, 1)
+        total[...] = sent[...] + self.side_y[...]
+        self.start(total.at[:, 1 - p.x], self.side_x, 2, p.sides()[0])
+
+    def step_x(self, total):
+        p = self.place
+        self.arrived(self.side_x, 2)
+        for z in range(4):
+            self.side_x[z] = self.side_x[z] + total[z, p.x]
+        for k in (1, 2, 3):
+            self.start(self.side_x.at[p.zs[k]], self.line.at[k - 1], 2 + k, p.to(z=p.zs[k]))
+
+    def step_line(self, out):
+        total = self.side_x[self.place.z]
+        for k in (1, 2, 3):
+            self.arrived(self.line.at[k - 1], 2 + k)
+            total = total + self.line[k - 1]
+        out[...] = total
 VMEM = pl.BlockSpec(memory_space=pltpu.VMEM)
 ANY = pl.BlockSpec(memory_space=pl.ANY)
 LIMIT = 61 * 1024 * 1024
@@ -554,6 +702,181 @@
         g.drain()
 
 
+def second_kernel(
+    linked, images, slots, width, hidden_width,
+    n2, n2t, dm, dmt, w_up, b_up, w_down, b_d, middle_in, live, gain2,
+    out, middle, d_low, g_up, g_down, g_b_up, g_g2, g_s2, g_bd, g_bo, act, dh, stack,
+):
+    middle[...] = middle_in[...]
+
+    def put_up(c, value):
+        if linked:
+            per = 2 * width // TILE
+            g_up[:, :, :, c // per, :, tile_at(lax.rem(c, per), TILE)] = value.reshape(4, 2, 2, 48, TILE)
+        else:
+            g_up[:, tile_at(c, TILE)] = value
+
+    def put_down(c, value):
+        if linked:
+            for j in range(2):
+                col = 2 * c + j
+                f = col // 3
+                g_down[f // 2, lax.rem(f, 2), :, :, :, tile_at(lax.rem(col, 3), 128)] = value[:, j * 128 : (j + 1) * 128].reshape(2, 2, 192, 128)
+        else:
+            g_down[:, tile_at(c, TILE)] = value
+
+    stage_mlp(width, hidden_width, n2, n2t, dm, dmt, w_up, b_up, w_down, act, dh, put_up, put_down, g_b_up)
+    stage_mlp_out(images, slots, width, act, dh, w_up, w_down, b_d, middle, live, gain2, dm, stack, out, d_low, g_g2, g_s2, g_bd, g_bo)
+
+
+def third_plain(
+    images, slots, width, d_low, att_t, w_out, qkv_in, probs, n1t, w_qkv, token, gain, mid, live, keep,
+    g_out, g_qkv, g_b, g_g1, g_s1, gp, stack, tile, flat, qkv,
+):
+    def put(ref, c, value):
+        ref[:, tile_at(c, TILE)] = value
+
+    def put_patches(i, value):
+        gp[i] = value
+
+    qkv[...] = qkv_in[...]
+    tile[...] = jnp.zeros_like(tile)
+    stage_out_back(width, att_t, d_low, w_out, functools.partial(put, g_out), stack)
+    for i in range(images):
+        stage_attention_back(width, qkv, probs.at[pl.ds(i * H, H)], stack, i, 0, H // 2)
+    stage_qkv_back(images, width, qkv, n1t, tile, flat, functools.partial(put, g_qkv), g_b, 0, 3 * width // TILE)
+    stage_norm_back(width, flat, w_qkv, stack)
+    stage_end(images, slots, width, keep, token, gain, mid, live, stack, g_g1, g_s1, put_patches)
+
+
+def third_kernel(
+    images, slots, width,
+    d_low, att_t, w_out, keep, gain, s_bup, s_g2, s_s2, s_bd, s_bo, h_qkv, h_probs, h_n1t, h_wqkv, h_token, h_mid, h_live, g_up, g_down,
+    gp, e_up, e_down, e_out, e_q, e_k, e_v, e_small,
+    stack, tile, flat, qkv, probs, n1t, w_qkv, token, mid, live, stage, g_b, g_g1, g_s1, g_attn,
+    up_held, up_core, up_dx, up_dy, up_sx, up_sy, up_ln, dn_held, dn_core, dn_dx, dn_dy, dn_sx, dn_sy, dn_ln,
+    core4, dx4, dy4, sx4, sy4, ln4, v_home, v_core, v_sy, v_sx, v_ln, v_sent, v_total,
+    send6, recv6, v_send, v_recv, own, probs_sem, out_sem,
+):
+    place = Place()
+    side_x, side_y, side_c = place.sides()
+    enter([place.to(z=place.zs[k]) for k in (1, 2, 3)] + [side_x, side_y, side_c])
+    r_up = Reduce(place, g_up, up_held, up_core, up_dx, up_dy, up_sx, up_sy, up_ln, e_up, send6.at[0], recv6.at[0])
+    r_down = Reduce(place, g_down, dn_held, dn_core, dn_dx, dn_dy, dn_sx, dn_sy, dn_ln, e_down, send6.at[1], recv6.at[1])
+    r_q, r_k, r_v, r_out = (
+        Reduce(place, g_attn.at[m], None, core4.at[m], dx4.at[m], dy4.at[m], sx4.at[m], sy4.at[m], ln4.at[m], e, send6.at[2 + m], recv6.at[2 + m])
+        for m, e in enumerate((e_q, e_k, e_v, e_out))
+    )
+    small = SmallReduce(place, v_home, v_core, v_sy, v_sx, v_ln, v_send, v_recv)
+    r_down.begin(pltpu.make_async_copy(g_down.at[:, :, place.c], dn_held, own.at[0]))
+    r_up.begin(pltpu.make_async_copy(g_up.at[:, :, place.c], up_held, own.at[1]))
+    fetch = {}
+    for j, (name, src, dst) in enumerate(
+        (("qkv", h_qkv, qkv), ("n1t", h_n1t, n1t), ("w_qkv", h_wqkv, w_qkv), ("token", h_token, token), ("mid", h_mid, mid), ("live", h_live, live))
+    ):
+        fetch[name] = pltpu.make_async_copy(src, dst, own.at[2 + j])
+
+    def load_probs(i):
+        return pltpu.make_async_copy(h_probs.at[pl.ds(i * H, H)], probs.at[i % 2], probs_sem.at[i % 2])
+
+    fetch["qkv"].start()
+    load_probs(0).start()
+    for name in ("n1t", "w_qkv", "token", "mid", "live"):
+        fetch[name].start()
+
+    def put(m, c, value):
+        for j in range(2):
+            col = 2 * c + j
+            y, off = lax.rem(col, 6) // 3, lax.rem(col, 3)
+            at = pl.ds(pl.multiple_of(off * 128, 128), 128)
+            g_attn[col // 6 if m is None else m, :, :, :, y, :, at] = value[:, j * 128 : (j + 1) * 128].reshape(4, 2, 2, 48, 128)
+
+    stage_out_back(width, att_t, d_low, w_out, functools.partial(put, 3), stack)
+    r_out.begin()
+    r_down.step_core()
+    r_up.step_core()
+    fetch["qkv"].wait()
+    steps = {
+        1: [r_out.step_core],
+        3: [r_down.step_diag],
+        6: [r_up.step_diag],
+        7: [r_out.step_diag],
+    }
+    for i in range(images):
+        load_probs(i).wait()
+        if i + 1 < images:
+            load_probs(i + 1).start()
+        for h in range(2):
+            stage_attention_back(width, qkv, probs.at[i % 2], stack, i, h * 3, h * 3 + 3)
+            for step in steps.get(2 * i + h, []):
+                step()
+    fetch["n1t"].wait()
+    tile[...] = jnp.zeros_like(tile)
+    back = functools.partial(stage_qkv_back, images, width, qkv, n1t, tile, flat, functools.partial(put, None), g_b)
+    third = width // TILE
+    back(0, third)
+    r_q.begin()
+    r_down.step_side()
+    back(third, 2 * third)
+    r_k.begin()
+    r_q.step_core()
+    back(2 * third, 3 * third)
+    r_v.begin()
+    r_k.step_core()
+    for name in ("w_qkv", "token", "mid", "live"):
+        fetch[name].wait()
+    stage_norm_back(width, flat, w_qkv, stack)
+    r_v.step_core()
+    r_up.step_side()
+    r_q.step_diag()
+    flights = []
+
+    def put_patches(i, value):
+        if i >= 2:
+            flights[i - 2].wait()
+        stage[i % 2] = value
+        copy = pltpu.make_async_copy(stage.at[i % 2], gp.at[i], out_sem.at[i % 2])
+        copy.start()
+        flights.append(copy)
+
+    stage_end(images, slots, width, keep, token, gain, mid, live, stack, g_g1, g_s1, put_patches)
+    v_home[...] = jnp.zeros_like(v_home)
+    for j, (ref, base) in enumerate(((g_g1, 0), (g_s1, 0), (g_b, 0), (g_b, 2 * width), (s_bo, 0), (s_g2, 0), (s_s2, 0), (s_bd, 0))):
+        row = ref[:, base : base + width]
+        for f in range(8):
+            v_home[f // 2, f % 2, j : j + 1, :96] = row[:, 96 * f : 96 * f + 96]
+    row = s_bup[...]
+    for f in range(8):
+        for j in range(4):
+            v_home[f // 2, f % 2, 8 + j : 9 + j, :96] = row[:, 384 * f + 96 * j : 384 * f + 96 * j + 96]
+    small.begin()
+    r_down.step_line()
+    r_k.step_diag()
+    small.step_core(v_sent)
+    r_out.step_side()
+    r_v.step_diag()
+    small.step_y(v_sent, v_total)
+    r_q.step_side()
+    r_up.step_line()
+    r_down.step_share()
+    small.step_x(v_total)
+    r_k.step_side()
+    r_out.step_line()
+    r_v.step_side()
+    r_up.step_share()
+    small.step_line(e_small)
+    for r in (r_q, r_k, r_v):
+        r.step_line()
+    for r in (r_out, r_q, r_k, r_v):
+        r.step_share()
+    for r in (r_down, r_up, r_out, r_q, r_k, r_v):
+        r.finish()
+    for copy in flights[-2:]:
+        copy.wait()
+    for r in (r_down, r_up, r_out, r_q, r_k, r_v, small):
+        r.drain()
+
+
 def shards(
     linked,
     patches, keep, ln1_gain, ln1_bias, w_qkv, b_query, b_value, w_out, b_out,
@@ -606,41 +929,71 @@
         )
     gain1, gain2, b_d = vectors[0:1], vectors[5:6], vectors[7:8]
 
-    def second(n2, n2t, dm, dmt, w_up, b_up, w_down, b_d, middle_in, live, gain2, out, middle, d_low, g_up, g_down_t, g_b_up, g_g2, g_s2, g_bd, g_bo, act, dh, stack):
-        middle[...] = middle_in[...]
-        stage_mlp(width, hidden_width, n2, n2t, dm, dmt, w_up, b_up, w_down, act, dh, g_up, g_down_t, g_b_up)
-        stage_mlp_out(images, slots, width, act, dh, w_up, w_down, b_d, middle, live, gain2, dm, stack, out, d_low, g_g2, g_s2, g_bd, g_bo)
-
     hid = ((ROWS, hidden_width), BF16)
-    out_tokens, d_mid, d_low, g_up, g_down_t, g_b_up, g_g2, g_s2, g_bd, g_bo = call(
-        second,
-        [((images, slots, width), BF16), rows_wide, rows_low, ((width, hidden_width), BF16), ((width, hidden_width), BF16), ((1, hidden_width), F32)] + [row_like] * 4,
+    if linked:
+        grads_like = [((4, 2, 2, 2, 48, 2 * width), BF16), ((4, 2, 2, 2, 192, width // 2), BF16)]
+    else:
+        grads_like = [((width, hidden_width), BF16)] * 2
+    out_tokens, d_mid, d_low, g_up, g_down, g_b_up, g_g2, g_s2, g_bd, g_bo = call(
+        functools.partial(second_kernel, linked, images, slots, width, hidden_width),
+        [((images, slots, width), BF16), rows_wide, rows_low] + grads_like + [((1, hidden_width), F32)] + [row_like] * 4,
         [hid, hid, rows_wide],
         (n2, n2t, dm, dmt, up_full, bias_up, down_full, b_d, middle, live, gain2),
         "second",
     )
-
-    def third(d_low, att_t, w_out, qkv, probs, n1t, w_qkv, token, gain1, d_mid, live, keep, g_out, g_qkv, g_b, g_g1, g_s1, gp, stack, tile, flat, d_qkv):
-        stage_out_back(width, att_t, d_low, w_out, g_out, stack)
-        stage_attention_back(images, width, qkv, probs, stack, d_qkv)
-        stage_qkv_back(images, width, d_qkv, n1t, w_qkv, tile, flat, g_qkv, g_b, stack)
-        stage_end(images, slots, width, keep, token, gain1, d_mid, live, stack, g_g1, g_s1, gp)
-
-    g_out, g_qkv, g_b, g_g1, g_s1, grad_patches = call(
-        third,
-        [((width, width), BF16), ((width, 3 * width), BF16), ((1, 3 * width), F32), row_like, row_like, ((images, slots, width), F32)],
-        [rows_wide, ((ROWS, TILE), F32), ((ROWS, 3 * width), BF16), heads_like],
-        (d_low, att_t, out_full, qkv, probs, n1t, qkv_full, token, gain1, d_mid, live, keep_pad),
-        "third",
-    )
-    both = ("fsdp", "dp")
-    scat = lambda v, dim=0: lax.psum(lax.psum_scatter(v, "fsdp", scatter_dimension=dim, tiled=True), "dp").astype(F32)
-    small = jnp.concatenate([g_g1, g_s1, g_b[:, :width], g_b[:, 2 * width :], g_bo, g_g2, g_s2, g_bd], axis=0).astype(BF16)
-    small = scat(small, 1)
-    b_up_sum = scat(g_b_up.astype(BF16), 1)[0]
+    if linked:
+        final = lambda r, w: ((2, 2, r, w), BF16)
+        attn = final(48, width // 2)
+        outs = [((images, slots, width), F32), final(48, 2 * width), final(192, width // 2), attn, attn, attn, attn, ((16, BLOCK), F32)]
+        half = width // 2
+
+        def buffers(r, w, by_rows, cut, lead=()):
+            other = (4, r - cut, w) if by_rows else (4, r, w - cut)
+            first = (4, cut, w) if by_rows else (4, r, cut)
+            shapes = [(4, 2, 2, r, w), other, first, (4, r, w), (4, r, w), (3, r, w)]
+            return [(lead + s, BF16) for s in shapes]
+
+        scratch = [rows_wide, ((ROWS, TILE), F32), ((ROWS, 3 * width), BF16), heads_like, ((2, H, SLOT, SLOT), BF16), cols_low]
+        scratch += [((width, 3 * width), BF16), rows_low, rows_wide, live_like, ((2, slots, width), F32), ((1, 3 * width), F32), row_like, row_like]
+        scratch += [((4, 4, 2, 2, 2, 48, half), BF16)]
+        scratch += [((4, 2, 2, 48, 2 * width), BF16)] + buffers(48, 2 * width, False, 512)
+        scratch += [((4, 2, 2, 192, half), BF16)] + buffers(192, half, True, 64)
+        scratch += buffers(48, half, False, 128, (4,))
+        small_like, line_like = ((4, 2, 16, BLOCK), F32), ((3, 16, BLOCK), F32)
+        scratch += [small_like, small_like, small_like, ((4, 16, BLOCK), F32), line_like, small_like, small_like]
+        grad_patches, e_up, e_down, e_out, e_q, e_k, e_v, small = pl.pallas_call(
+            functools.partial(third_kernel, images, slots, width),
+            out_shape=[jax.ShapeDtypeStruct(*o) for o in outs],
+            in_specs=[VMEM] * 10 + [ANY] * 9,
+            out_specs=[ANY] + [VMEM] * 7,
+            scratch_shapes=[pltpu.VMEM(*s) for s in scratch]
+            + [pltpu.SemaphoreType.DMA((6, 10))] * 2
+            + [pltpu.SemaphoreType.DMA((6,))] * 2
+            + [pltpu.SemaphoreType.DMA((8,)), pltpu.SemaphoreType.DMA((2,)), pltpu.SemaphoreType.DMA((2,))],
+            compiler_params=pltpu.CompilerParams(vmem_limit_bytes=LIMIT, collective_id=1, has_side_effects=True),
+            name="third",
+        )(d_low, att_t, out_full, keep_pad, gain1, g_b_up, g_g2, g_s2, g_bd, g_bo, qkv, probs, n1t, qkv_full, token, d_mid, live, g_up, g_down)
+        rows = small[:8, :part]
+        square = lambda e: e.transpose(0, 2, 1, 3).reshape(part, -1).astype(F32)
+        sum_qkv = jnp.concatenate([square(e) for e in (e_q, e_k, e_v)], axis=1)
+        sum_out, sum_up, sum_down = square(e_out), square(e_up), e_down.reshape(width, half).T.astype(F32)
+        b_up_sum = small[8:12, :part].reshape(-1)
+    else:
+        g_out, g_qkv, g_b, g_g1, g_s1, grad_patches = call(
+            functools.partial(third_plain, images, slots, width),
+            [((width, width), BF16), ((width, 3 * width), BF16), ((1, 3 * width), F32), row_like, row_like, ((images, slots, width), F32)],
+            [rows_wide, ((ROWS, TILE), F32), ((ROWS, 3 * width), BF16), heads_like],
+            (d_low, att_t, out_full, qkv, probs, n1t, qkv_full, token, gain1, d_mid, live, keep_pad),
+            "third",
+        )
+        scat = lambda v, dim=0: lax.psum(lax.psum_scatter(v, "fsdp", scatter_dimension=dim, tiled=True), "dp").astype(F32)
+        rows = jnp.concatenate([g_g1, g_s1, g_b[:, :width], g_b[:, 2 * width :], g_bo, g_g2, g_s2, g_bd], axis=0).astype(BF16)
+        rows = scat(rows, 1)
+        b_up_sum = scat(g_b_up.astype(BF16), 1)[0]
+        sum_qkv, sum_out, sum_up, sum_down = scat(g_qkv), scat(g_out), scat(g_up), scat(g_down, 1).T
     return (
-        out_tokens, grad_patches, small[0], small[1], scat(g_qkv), small[2], small[3], scat(g_out), small[4],
-        small[5], small[6], scat(g_up), b_up_sum, scat(g_down_t, 1).T, small[7],
+        out_tokens, grad_patches, rows[0], rows[1], sum_qkv, rows[2], rows[3], sum_out, rows[4],
+        rows[5], rows[6], sum_up, b_up_sum, sum_down, rows[7],
     )
 
 

time: 711 us -> 272 us (0.38)
  waiting for transfers between devices: 453 us -> 0 us
  Pallas kernels: 209 us -> 251 us
  between operations: 14.3 us -> 0.77 us
  blocking collectives: 7.55 us -> 0 us
    reduce_scatter x3 -> x0, waiting for transfers between devices: 246 us -> none  [shards(): lax.psum_scatter(v, 'fsdp', scatter_dimension=dim, tiled=True)]
    unnamed x10 -> x0, waiting for transfers between devices: 166 us -> none
    pallas_call x0 -> x1, Pallas kernels: none -> 95 us  [shards(): pl.pallas_call(functools.partial(third_kernel, images, slots, width), out...]
    pallas_call x2 -> x1, Pallas kernels: 111 us -> 57.9 us  [call(): pl.pallas_call(body, out_shape=[jax.ShapeDtypeStruct(*o) for o in outs],...]
    psum x1 -> x0, waiting for transfers between devices: 41.4 us -> none  [shards(): lax.psum(lax.psum_scatter(v, 'fsdp', scatter_dimension=dim, tiled=True),...]
    unnamed x26 -> x12, local copies, waits for them, and re-layouts: 14.1 us -> 5.73 us
    psum x1 -> x0, blocking collectives: 7.55 us -> none  [shards(): lax.psum(lax.psum_scatter(v, 'fsdp', scatter_dimension=dim, tiled=True),...]
  transfers between devices with their start and end apart: 7 -> 0, of which waited for: 7 -> 0; matrix products, arithmetic and copies ran while one was open for 1% -> 0% of each run, Pallas kernels for 8% -> 0%
where the time goes in v2:
time: 272 us
  Pallas kernels  251 us (92%)
  local copies, waits for them, and re-layouts  19.1 us (7%)
    pallas_call x1, Pallas kernels, shards(): pl.pallas_call(functools.partial(first_kernel, images, slots, width), out...  98.1 us
    pallas_call x1, Pallas kernels, shards(): pl.pallas_call(functools.partial(third_kernel, images, slots, width), out...  95 us
    pallas_call x1, Pallas kernels, call(): pl.pallas_call(body, out_shape=[jax.ShapeDtypeStruct(*o) for o in outs],...  57.9 us
    unnamed x12, local copies, waits for them, and re-layouts  5.73 us

profile of v2, /device:TPU:1, one launch (start us, length us, event | category | flops | bytes accessed | tf_op | source)
XLA Modules:
  0.0 272.0 jit_solution(16004066740830538240)
XLA Ops:
  0.6 0.8 reshape.90
  1.4 0.8 concatenate.9
  2.2 0.6 pad.9.vec
  2.8 0.7 pad.8
  3.5 0.6 reshape.81.keep
  4.1 98.1 %first.1 = (bf16[1024,768]{1,0:T(8,128)(2,1)}, bf16[768,1024]{1,0:T(8,128)(2,1)}, bf16[1024,768]{1,0:T(8,128)(2,1)}, bf16[768,1024]{1,0:T(8,128)(2,1)}, f32[1024...) custom-call(bf16[5,197,768]{2,1,0:T(8,128)(2,1)} %patches.1, ...), custom_call_target="tpu_custom_call" | custom-call | tf_op jit(solution)/shard_map/first/pallas_call | solution.py:907
  102.2 1.5 fusion
  103.7 57.9 %second.1 = (bf16[5,197,768]{2,1,0:T(8,128)(2,1)}, f32[1024,768]{1,0:T(8,128)}, bf16[1024,768]{1,0:T(8,128)(2,1)}, bf16[4,2,2,2,48,1536]{5,4,3,2,1,0:T(8,128)(2,...) custom-call(bf16[1024,768]{1,0:T(8,128)(2,1)} %get-tuple-element.50., ...), custom_call_target="tpu_custom_call" | custom-call | tf_op jit(solution)/shard_map/second/pallas_call | solution.py:595
  161.5 95.0 %third.1 = (f32[5,197,768]{2,1,0:T(8,128)}, bf16[2,2,48,1536]{3,2,1,0:T(8,128)(2,1)}, bf16[2,2,192,384]{3,2,1,0:T(8,128)(2,1)}, bf16[2,2,48,384]{3,2,1,0:T(8,128...) custom-call(bf16[1024,768]{1,0:T(8,128)(2,1)} %get-tuple-element.61., ...), custom_call_target="tpu_custom_call" | custom-call | tf_op jit(solution)/shard_map/third/pallas_call | solution.py:964
  256.5 0.0 copy-start.2
  256.5 1.1 copy.32
  257.6 0.7 slice.55
  258.3 1.5 slice_bitcast_fusion
  259.8 0.7 reshape.91
  260.5 1.0 copy.33
  261.5 1.0 copy.34
  262.6 0.0 copy-start.1
  262.6 0.0 copy-done.2
  262.6 0.2 copy.35
  262.8 0.7 copy.41
  263.5 1.0 maximum_convert_fusion
  264.5 0.0 copy-done.1
  264.5 0.1 convert_bitcast_fusion
  264.6 0.9 copy.36
  265.6 0.0 copy-start
  265.6 1.2 copy.42
  266.8 0.0 copy-done
  266.8 0.1 bitcast_convert_fusion
  266.9 1.4 copy.37
  268.3 3.7 %copy.44 = f32[5,197,768]{2,1,0:T(8,128)} copy(f32[5,197,768]{2,1,0:T(8,128)} %get-tuple-element.112) | data formatting | bytes 6051840
  (4 shorter events, 0.1 us)
Async XLA Ops:
  256.5 6.1 %copy-start.2 = (bf16[2,2,48,384]{3,2,1,0:T(8,128)(2,1)S(1)}, bf16[2,2,48,384]{3,2,1,0:T(8,128)(2,1)}, u32[]{:S(2)}) copy-start(bf16[2,2,48,384]{3,2,1,0:T(8,128)(2,1)} %get-tuple-element.82) | copy-start | bytes 442372
  262.6 1.9 copy-start.1
  265.6 1.2 copy-start
